TPU v7x, 128 devices: a whole 4x4x4 slice. The times are simulated.
128 devices in a mesh: seq: 8 (over z, core), batch: 16 (over x, y).
Axes of the slice: x: 4, y: 4, z: 4, core: 2. Of those that a mesh axis runs over, the one named last changes fastest.
Arguments:
- queries: bfloat16 [16, 4096, 2048], P('batch', 'seq'), may hold values from -6 to 6
- keys: bfloat16 [16, 4096, 2048], P('batch', 'seq'), may hold values from -6 to 6
- values: bfloat16 [16, 4096, 2048], P('batch', 'seq'), may hold values from -6 to 6
- level_gain: float32 [16, 4096, 128], P('batch', 'seq'), may hold values from 0.004 to 0.06
- out_weight: bfloat16 [2048, 2048], P('batch'), may hold values from -0.125 to 0.125
- out_grad: bfloat16 [16, 4096, 2048], P('batch', 'seq'), may hold values from -6 to 6
Outputs:
- query_grad: bfloat16 [16, 4096, 2048], P('batch', 'seq')
- key_grad: bfloat16 [16, 4096, 2048], P('batch', 'seq')
- value_grad: bfloat16 [16, 4096, 2048], P('batch', 'seq')
- gain_grad: float32 [16, 4096, 128], P('batch', 'seq')
- weight_grad: float32 [2048, 2048], P(('seq', 'batch'))
All inputs are finite; a program needn't handle non-finite values.
Results may differ from a plain program's by a relative error of at most 0.0064.
Values may be sent and summed in bfloat16 or wider, within the bound.
A program may use at most 192 MiB of HBM per device.

v0:
```python
import jax
import jax.numpy as jnp
import numpy as np
from jax import lax
from jax.sharding import PartitionSpec as P

H = 16
HD = 128
GROUP = 64
LEVELS = 8


def swapped(value, axis, stride):
    mask = 2**stride
    pairs = [(source, source ^ mask) for source in range(lax.axis_size(axis))]
    return lax.ppermute(value, axis, pairs)


def in_blocks(value, dim, length):
    before, after = (value.shape[:dim], value.shape[dim + 1 :])
    return jnp.moveaxis(value.reshape(*before, length, -1, *after), dim, 0)


def summed_on_arrival(value, axis, dim):
    parts = in_blocks(value, dim, lax.axis_size(axis))
    arrived = lax.all_to_all(parts, axis, split_axis=0, concat_axis=0, tiled=True)
    return arrived.sum(axis=0)


def level_selects(seg_len):
    loc_bits = (seg_len // GROUP).bit_length() - 1
    position = np.arange(seg_len, dtype=np.int32)
    group_id = position // GROUP
    crossed = group_id[:, None] ^ group_id[None, :]
    level_id = np.zeros((seg_len, seg_len), np.int32)
    for shift_bit in range(loc_bits):
        level_id = level_id + (crossed >> shift_bit > 0).astype(np.int32)
    causal = position[None, :] <= position[:, None]
    return [
        jnp.asarray(((level_id == level_num) & causal).astype(np.float32), jnp.float32)
        for level_num in range(loc_bits + 1)
    ]


def local(queries, keys, values, level_gain, out_weight, out_grad):
    seg_len = queries.shape[1]
    width = queries.shape[2]
    highest = lax.Precision.HIGHEST
    score_scale = HD ** (-0.5)
    seq_count = lax.axis_size("seq")
    n_bits = seq_count.bit_length() - 1
    seg_index = lax.axis_index("seq")
    selects = level_selects(seg_len)
    loc_bits = len(selects) - 1
    grad_rows = out_grad[0]
    attn_grad = lax.dot_general(
        grad_rows,
        lax.all_gather(out_weight, "batch", axis=0, tiled=True),
        (((1,), (1,)), ((), ())),
        preferred_element_type=jnp.float32,
    ).astype(jnp.bfloat16)
    query_heads = queries[0].reshape(seg_len, H, HD)
    key_heads = keys[0].reshape(seg_len, H, HD)
    value_heads = values[0].reshape(seg_len, H, HD)
    grad_heads = attn_grad.reshape(seg_len, H, HD)
    gains = level_gain[0].reshape(seg_len, LEVELS, H)
    own_bits = [(seg_index >> level_bit & 1).astype(jnp.float32) for level_bit in range(n_bits)]
    states = jnp.einsum("thd,the->hde", key_heads, value_heads, preferred_element_type=jnp.float32)
    running = states
    far_list = []
    for level_bit in range(n_bits):
        received = swapped(running, "seq", level_bit)
        far_list.append(received * own_bits[level_bit])
        running = running + received
    far_stack = jnp.stack(far_list)
    far_half = far_stack.astype(jnp.bfloat16)
    scores = (
        jnp.einsum("thd,shd->hts", query_heads, key_heads, preferred_element_type=jnp.float32)
        * score_scale
    )
    weight_mask = jnp.zeros((H, seg_len, seg_len), jnp.float32)
    for level_num in range(loc_bits + 1):
        weight_mask = weight_mask + selects[level_num][None] * gains[:, level_num, :].T[:, :, None]
    probs = (scores * weight_mask).astype(jnp.bfloat16)
    intra = jnp.einsum("hts,shd->thd", probs, value_heads, preferred_element_type=jnp.float32)
    far_gain = jnp.transpose(gains[:, loc_bits + 1 : loc_bits + 1 + n_bits, :], (1, 0, 2))
    projected = (
        jnp.einsum("thd,bhde->bthe", query_heads, far_half, preferred_element_type=jnp.float32)
        * score_scale
    )
    cross = jnp.sum(far_gain[..., None] * projected, axis=0)
    attn = (intra + cross).reshape(seg_len, width).astype(jnp.bfloat16)
    seq_part = lax.psum_scatter(
        lax.dot_general(
            attn, grad_rows, (((0,), (0,)), ((), ())), preferred_element_type=jnp.float32
        ),
        "seq",
        scatter_dimension=0,
        tiled=True,
    )
    weight_grad = summed_on_arrival(seq_part, "batch", 0)
    prob_grad = jnp.einsum(
        "thd,shd->hts", grad_heads, value_heads, preferred_element_type=jnp.float32
    )
    grad_v_in = jnp.einsum("hts,thd->shd", probs, grad_heads, preferred_element_type=jnp.float32)
    energy = prob_grad * scores
    local_gain = jnp.stack(
        [jnp.sum(energy * sel_mat[None], axis=2).T for sel_mat in selects], axis=1
    )
    score_grad = (prob_grad * weight_mask).astype(jnp.bfloat16)
    grad_q_in = (
        jnp.einsum("hts,shd->thd", score_grad, key_heads, preferred_element_type=jnp.float32)
        * score_scale
    )
    grad_k_in = (
        jnp.einsum("hts,thd->shd", score_grad, query_heads, preferred_element_type=jnp.float32)
        * score_scale
    )
    weighted = (far_gain[..., None] * grad_heads[None]).astype(jnp.bfloat16)
    grad_q_far = (
        jnp.einsum("bthe,bhde->thd", weighted, far_half, preferred_element_type=jnp.float32)
        * score_scale
    )
    cross_gain = jnp.transpose(jnp.sum(projected * grad_heads[None], axis=3), (1, 0, 2))
    weighted_query = (far_gain[..., None] * query_heads[None]).astype(jnp.bfloat16)
    far_grad = (
        jnp.einsum("bthd,the->bhde", weighted_query, grad_heads, preferred_element_type=jnp.float32)
        * score_scale
    )
    far_grad = far_grad * jnp.stack(own_bits)[:, None, None, None]
    target = jnp.arange(1 * lax.axis_size("seq"), dtype=jnp.int32)
    member_cols = []
    for level_bit in range(n_bits):
        member = (target >> level_bit & 1 == 0) & (
            target >> level_bit + 1 == seg_index >> level_bit + 1
        )
        member_cols.append(member.astype(jnp.float32))
    weights = jnp.stack(member_cols, axis=1)
    state_grad = lax.psum_scatter(
        jnp.einsum("nb,bhde->nhde", weights, far_grad, precision=highest),
        "seq",
        scatter_dimension=0,
        tiled=True,
    )[0]
    state_half = state_grad.astype(jnp.bfloat16)
    grad_k = grad_k_in + jnp.einsum(
        "she,hde->shd", value_heads, state_half, preferred_element_type=jnp.float32
    )
    grad_v = grad_v_in + jnp.einsum(
        "shd,hde->she", key_heads, state_half, preferred_element_type=jnp.float32
    )
    spare = LEVELS - loc_bits - 1 - n_bits
    gain_grad = jnp.concatenate(
        [local_gain, cross_gain, jnp.zeros((seg_len, spare, H), jnp.float32)], axis=1
    )
    query_grad = (grad_q_in + grad_q_far).reshape(seg_len, width).astype(jnp.bfloat16)
    key_grad = grad_k.reshape(seg_len, width).astype(jnp.bfloat16)
    value_grad = grad_v.reshape(seg_len, width).astype(jnp.bfloat16)
    return (
        query_grad[None],
        key_grad[None],
        value_grad[None],
        gain_grad.reshape(seg_len, LEVELS * H)[None],
        weight_grad,
    )


def solution(mesh):
    placed = (
        P("batch", "seq", None),
        P("batch", "seq", None),
        P("batch", "seq", None),
        P("batch", "seq", None),
        P("batch", None),
        P("batch", "seq", None),
    )
    return jax.shard_map(
        local,
        mesh=mesh,
        in_specs=placed,
        out_specs=(
            P("batch", "seq", None),
            P("batch", "seq", None),
            P("batch", "seq", None),
            P("batch", "seq", None),
            P(("seq", "batch"), None),
        ),
        check_vma=False,
    )
```

profile of v0, /device:TPU:1, one launch (start us, length us, event | category | flops | bytes accessed | tf_op | source)
XLA Modules:
  0.0 317.0 jit_solution(10061984979363459074)
XLA Ops:
  7.2 0.7 all-gather.2.cloned.1.call-update
  8.0 3.5 %copy.125 = bf16[64,8,16,128]{3,2,1,0:T(8,128)(2,1)} copy(bf16[64,8,16,128]{3,1,2,0:T(8,128)(2,1)} %bitcast.142) | data formatting | bytes 4194304
  11.5 3.9 %copy.124 = bf16[1,512,2048]{1,2,0:T(8,128)(2,1)} copy(bf16[1,512,2048]{2,1,0:T(8,128)(2,1)} %param.12) | data formatting | bytes 4194304 | tf_op jit(solution)/shard_map/reshape;squeeze | solution.py:64
  15.4 3.5 %fusion.28 = f32[16,128,128]{2,1,0:T(8,128)S(1)} fusion(bf16[512,16,128]{0,2,1:T(8,128)(2,1)} %bitcast.136, bf16[512,16,128]{2,1,0:T(8,128)(2,1)} %bitcast.127), kind=kOutput, calls=%fused_computation.43 | convolution fusion | flops 268435456 | bytes 5242880 | tf_op jit(solution)/shard_map/thd,the->hde/dot_general | solution.py:68
  19.0 1.5 collective-permute-start
  20.5 2.4 collective-permute-done
  22.9 2.6 fusion.34
  25.5 1.7 collective-permute-start.1
  27.4 23.4 %collective-permute-done.1 = f32[16,128,128]{2,1,0:T(8,128)} collective-permute-done((f32[16,128,128]{2,1,0:T(8,128)}, f32[16,128,128]{2,1,0:T(8,128)}, u32[]{:S(2)}, u32[]{:S(2)}) %collective-permute-start.1) | collective-permute-done | bytes 1048608 | tf_op jit(solution)/shard_map/ppermute | solution.py:16
  50.8 2.9 fusion.35
  53.7 3.1 collective-permute-start.2
  56.8 2.4 copy.127
  59.9 8.4 %fusion.20 = f32[16,512,512]{1,2,0:T(8,128)} fusion(bf16[512,16,128]{2,1,0:T(8,128)(2,1)S(1)} %bitcast.131, bf16[512,16,128]{2,1,0:T(8,128)(2,1)S(1)} %bitcast.128), kind=kOutput, calls=%fused_computation.38 | convolution fusion | flops 1073741824 | bytes 20971520 | tf_op jit(solution)/shard_map/thd,shd->hts/dot_general | solution.py:78
  68.3 11.1 %collective-permute-done.2 = f32[16,128,128]{2,1,0:T(8,128)} collective-permute-done((f32[16,128,128]{2,1,0:T(8,128)}, f32[16,128,128]{2,1,0:T(8,128)}, u32[]{:S(2)}, u32[]{:S(2)}) %collective-permute-start.2) | collective-permute-done | bytes 1048608 | tf_op jit(solution)/shard_map/ppermute | solution.py:16
  79.3 2.2 fusion.36
  81.5 2.5 all-gather.2.cloned.1.call-done
  84.0 8.6 %fusion.24 = bf16[64,8,16,128]{3,1,2,0:T(8,128)(2,1)S(1)} fusion(bf16[2048,2048]{1,0:T(8,128)(2,1)} %all-gather.2.cloned.1.call-done, bf16[1,512,2048]{2,1,0:T(8,128)(2,1)S(1)} %copy-done), kind=kOutput, calls=%fused_computation.40 | convolution fusion | flops 4296015872 | bytes 12582912 | tf_op jit(solution)/shard_map/dot_general | solution.py:56
  93.3 1.3 copy-done.7
  94.6 2.5 broadcast_multiply_fusion
  97.0 4.3 %copy.95 = bf16[512,16,128]{0,2,1:T(8,128)(2,1)} copy(bf16[512,16,128]{2,1,0:T(8,128)(2,1)} %bitcast.134) | data formatting | bytes 4194304 | tf_op jit(solution)/shard_map/reshape | solution.py:65
  101.4 5.4 %copy.101 = f32[512,16,128]{0,2,1:T(8,128)} copy(f32[512,16,128]{2,1,0:T(8,128)} %broadcast_multiply_fusion) | data formatting | bytes 8388608 | tf_op jit(solution)/shard_map/mul | solution.py:124
  106.7 7.3 %fusion.1 = (f32[512,16,128]{0,2,1:T(8,128)S(1)}, f32[3,512,16]{1,0,2:T(4,128)S(1)}) fusion(f32[3,512,16]{1,0,2:T(4,128)S(1)} %copy.105, f32[512,16,128]{0,2,1:T(8,128)} %copy.101, bf16[512,16,128,1]{2,1,0,3:T(8,128)(2,1)} %bitcast.132, bf16[1,16,128,128]{3,2,1,0:T(8,128)(2,1)} %fusion.36, bf16[1,16,128,128]{3,2,1,0:T(8,128)(2,1)} %get-tuple-element.31, ...), kind=kOutput, calls=%fused_computation.11 | convolution fusion | flops 818388992 | bytes 12255232 | tf_op jit(solution)/shard_map/thd,bhde->bthe/dot_general | solution.py:88
  114.0 18.0 %multiply_multiply_fusion = (f32[16,512,512]{1,2,0:T(8,128)}, bf16[16,512,512]{1,2,0:T(8,128)(2,1)S(1)}, bf16[16,512,512]{1,2,0:T(8,128)(2,1)}) fusion(f32[16,512,512]{1,2,0:T(8,128)} %fusion.20, f32[16,512]{1,0:T(8,128)} %get-tuple-element.34, f32[512,512]{0,1:T(8,128)} %constant.9.clone, f32[16,512]{1,0:T(8,128)} %get-tuple-element.35, ...), kind=kOutput, calls=%fused_computation.7 | convolution fusion | flops 1128267776 | bytes 58851328 | tf_op jit(solution)/shard_map/thd,shd->hts/dot_general | solution.py:102
  132.0 1.3 fusion.7
  133.3 1.9 copy-done.9
  135.2 8.2 %fusion.15 = f32[2048,2048]{1,0:T(8,128)} fusion(bf16[512,2048]{0,1:T(8,128)(2,1)S(1)} %bitcast.146, bf16[1,512,2048]{2,1,0:T(8,128)(2,1)S(1)} %copy-done), kind=kOutput, calls=%fused_computation.32 | convolution fusion | flops 4294967296 | bytes 20971520 | tf_op jit(solution)/shard_map/dot_general | solution.py:94
  143.5 1.4 copy-done.5
  145.4 1.4 copy.88
  147.0 7.0 %multiply_bitcast_fusion = f32[3,16,128,128]{2,3,0,1:T(8,128)} fusion(f32[512,16,128]{2,0,1:T(8,128)S(1)} %copy.88, f32[3,512,16]{1,0,2:T(4,128)S(1)} %copy.83, bf16[512,16,128,1]{2,1,0,3:T(8,128)(2,1)S(1)} %bitcast.135, f32[3]{0:T(128)S(1)} %maximum_multiply_fusion), kind=kOutput, calls=%fused_computation.27 | convolution fusion | flops 812384256 | bytes 9535500 | tf_op jit(solution)/shard_map/bthd,the->bhde/dot_general | solution.py:127
  154.0 5.0 %copy.90 = f32[3,16,128,128]{3,0,2,1:T(4,128)} copy(f32[3,16,128,128]{2,3,0,1:T(8,128)} %multiply_bitcast_fusion) | data formatting | bytes 6291456 | tf_op jit(solution)/shard_map/mul | solution.py:130
  159.0 6.8 %fusion.41 = f32[8,16,128,128]{3,0,2,1:T(8,128)S(1)} fusion(f32[3,16,128,128]{3,0,2,1:T(4,128)} %copy.90, pred[8,1]{0,1:T(4,128)(4,1)S(1)} %get-tuple-element.37, pred[8,1]{0,1:T(4,128)(4,1)S(1)} %get-tuple-element.38, pred[8,1]{0,1:T(4,128)(4,1)S(1)} %compare_and_fusion.2), kind=kOutput, calls=%fused_computation.66 | convolution fusion | flops 75497520 | bytes 11534360 | tf_op jit(solution)/shard_map/nb,bhde->nhde/dot_general | solution.py:140
  165.8 4.7 %copy.91 = f32[8,16,128,128]{3,2,1,0:T(8,128)} copy(f32[8,16,128,128]{3,0,2,1:T(8,128)S(1)} %fusion.41) | data formatting | bytes 16777216 | tf_op jit(solution)/shard_map/nb,bhde->nhde/dot_general | solution.py:140
  171.1 3.2 %copy.84 = f32[512,16,128]{2,0,1:T(8,128)} copy(f32[512,16,128]{2,1,0:T(8,128)S(1)} %bitcast_convert_fusion.1) | data formatting | bytes 8388608 | tf_op jit(solution)/shard_map/convert_element_type | solution.py:119
  174.3 9.2 %multiply_reduce_fusion = (f32[16,512]{1,0:T(8,128)S(1)}, f32[16,512]{1,0:T(8,128)S(1)}, f32[16,512]{1,0:T(8,128)S(1)}, f32[16,512]{1,0:T(8,128)S(1)}) fusion(f32[16,512,512]{1,2,0:T(8,128)} %get-tuple-element.26, f32[512,512]{0,1:T(8,128)S(1)} %copy-done.14, f32[512,512]{0,1:T(8,128)S(1)} %copy-done.15, f32[512,512]{0,1:T(8,128)S(1)} %copy-done.16, ...), kind=kLoop, calls=%fused_computation | loop fusion | flops 33521664 | bytes 21102592 | tf_op jit(solution)/shard_map/reduce_sum | solution.py:108
  184.2 0.8 copy.109
  185.0 5.4 %fusion.30 = f32[16,512,128]{1,2,0:T(8,128)S(1)} fusion(bf16[16,512,512]{1,2,0:T(8,128)(2,1)} %get-tuple-element.28, bf16[512,16,128]{2,1,0:T(8,128)(2,1)S(1)} %bitcast.129), kind=kOutput, calls=%fused_computation.45 | convolution fusion | flops 1073741824 | bytes 14680064 | tf_op jit(solution)/shard_map/hts,shd->thd/dot_general | solution.py:112
  190.4 6.3 %fusion.9 = bf16[512,16,128]{0,2,1:T(8,128)(2,1)} fusion(f32[16,512,128]{1,2,0:T(8,128)S(1)} %fusion.30, bf16[1,16,128,128]{3,2,1,0:T(8,128)(2,1)S(1)} %copy-done.18, bf16[1,16,128,128]{3,2,1,0:T(8,128)(2,1)S(1)} %copy-done.20, bf16[1,16,128,128]{3,2,1,0:T(8,128)(2,1)S(1)} %copy-done.19, f32[512,16,128]{2,0,1:T(8,128)S(1)} %copy-done.13, ...), kind=kOutput, calls=%fused_computation.24 | convolution fusion | flops 817364992 | bytes 12156928 | tf_op jit(solution)/shard_map/bthe,bhde->thd/dot_general | solution.py:121
  196.8 3.9 %copy.106 = bf16[1,512,2048]{2,1,0:T(8,128)(2,1)} copy(bf16[1,512,2048]{1,2,0:T(8,128)(2,1)} %bitcast.145) | data formatting | bytes 4194304
  200.7 34.6 %reduce-scatter.5.cloned.1.call-done = f32[256,2048]{1,0:T(8,128)} async-done(((f32[2048,2048]{1,0:T(8,128)}), f32[256,2048]{1,0:T(8,128)}) %reduce-scatter.5.cloned.1.call-update) | async-done | bytes 2097168 | tf_op jit(solution)/shard_map/reduce_scatter | solution.py:93
  235.3 6.8 %all-to-all-start = ((f32[16,16,2048]{2,1,0:T(8,128)}), f32[16,16,2048]{2,1,0:T(8,128)}, u32[]{:S(2)}, u32[]{:S(2)}) async-start(f32[16,16,2048]{2,1,0:T(8,128)} %bitcast.144), calls=%async_computation.2 | async-start | bytes 4194304 | tf_op jit(solution)/shard_map/all_to_all | solution.py:26
  242.1 8.9 %fusion.47 = f32[16,128,512]{2,1,0:T(8,128)} fusion(bf16[512,16,128]{0,2,1:T(8,128)(2,1)} %copy.95, bf16[16,512,512]{1,2,0:T(8,128)(2,1)} %copy-done.9), kind=kOutput, calls=%fused_computation.80 | convolution fusion | flops 1073741824 | bytes 14680064 | tf_op jit(solution)/shard_map/hts,thd->shd/dot_general | solution.py:105
  251.1 8.4 %fusion.18 = f32[16,512,128]{1,2,0:T(8,128)} fusion(bf16[16,512,512]{1,2,0:T(8,128)(2,1)} %get-tuple-element.28, bf16[512,16,128]{2,1,0:T(8,128)(2,1)S(1)} %bitcast.133), kind=kOutput, calls=%fused_computation.36 | convolution fusion | flops 1073741824 | bytes 14680064 | tf_op jit(solution)/shard_map/hts,thd->shd/dot_general | solution.py:116
  259.5 30.4 %reduce-scatter.3.cloned.1.call-done = f32[1,16,128,128]{3,2,1,0:T(8,128)} async-done(((f32[8,16,128,128]{3,2,1,0:T(8,128)}), f32[1,16,128,128]{3,2,1,0:T(8,128)}) %reduce-scatter.3.cloned.1.call-update) | async-done | bytes 1048592 | tf_op jit(solution)/shard_map/reduce_scatter | solution.py:139
  289.9 5.2 %add_convert_fusion = bf16[16,128,512]{2,1,0:T(8,128)(2,1)} fusion(f32[16,128,512]{2,1,0:T(8,128)} %fusion.47, bf16[512,16,128]{2,1,0:T(8,128)(2,1)S(1)} %bitcast.130, f32[1,16,128,128]{3,2,1,0:T(8,128)} %reduce-scatter.3.cloned.1.call-done), kind=kOutput, calls=%fused_computation.26 | convolution fusion | flops 270794752 | bytes 9437184 | tf_op jit(solution)/shard_map/shd,hde->she/dot_general | solution.py:149
  295.0 4.0 %copy.108 = bf16[1,512,2048]{2,1,0:T(8,128)(2,1)} copy(bf16[1,512,2048]{1,2,0:T(8,128)(2,1)} %bitcast.141) | data formatting | bytes 4194304
  299.0 5.0 %fusion.8 = bf16[512,16,128]{0,2,1:T(8,128)(2,1)} fusion(f32[16,512,128]{1,2,0:T(8,128)} %fusion.18, bf16[512,16,128]{0,2,1:T(8,128)(2,1)} %bitcast.137, f32[1,16,128,128]{3,2,1,0:T(8,128)S(1)} %copy-done.12), kind=kOutput, calls=%fused_computation.22 | convolution fusion | flops 271843328 | bytes 9437184 | tf_op jit(solution)/shard_map/she,hde->shd/dot_general | solution.py:146
  304.0 3.9 %copy.107 = bf16[1,512,2048]{2,1,0:T(8,128)(2,1)} copy(bf16[1,512,2048]{1,2,0:T(8,128)(2,1)} %bitcast.140) | data formatting | bytes 4194304
  307.9 2.4 reduce_sum.69
  (66 shorter events, 3.6 us)
Async XLA Ops:
  7.2 76.9 %copy-start = (bf16[1,512,2048]{2,1,0:T(8,128)(2,1)S(1)}, bf16[1,512,2048]{2,1,0:T(8,128)(2,1)}, u32[]{:S(2)}) copy-start(bf16[1,512,2048]{2,1,0:T(8,128)(2,1)} %param.15) | copy-start | bytes 6291460
  7.2 76.8 %all-gather.2.cloned.1.call-start = ((), (), s32[]{:S(2)}) async-start(), calls=%async_computation.3 | async-start | bytes 8912896 | tf_op jit(solution)/shard_map/all_gather | solution.py:58
  7.9 227.4 %reduce-scatter.5.cloned.1.call-start = ((), (), s32[]{:S(2)}) async-start(), calls=%async_computation.5 | async-start | bytes 18874368 | tf_op jit(solution)/shard_map/reduce_scatter | solution.py:93
  15.4 11.8 %copy-start.21 = (f32[1,512,128]{2,1,0:T(8,128)S(1)}, f32[1,512,128]{2,1,0:T(8,128)}, u32[]{:S(2)}) copy-start(f32[1,512,128]{2,1,0:T(8,128)} %param.13) | copy-start | bytes 786436
  19.0 3.9 %collective-permute-start = (f32[16,128,128]{2,1,0:T(8,128)S(1)}, f32[16,128,128]{2,1,0:T(8,128)}, u32[]{:S(2)}, u32[]{:S(2)}) collective-permute-start(f32[16,128,128]{2,1,0:T(8,128)S(1)} %fusion.28), channel_id=1, source_target_pairs={{0,16},{16,0},{32,48},{48,32},{64,80},{80,64},{96,112},{112,96},{1... | collective-permute-start | bytes 3145736 | tf_op jit(solution)/shard_map/ppermute | solution.py:16
  25.5 25.2 %collective-permute-start.1 = (f32[16,128,128]{2,1,0:T(8,128)}, f32[16,128,128]{2,1,0:T(8,128)}, u32[]{:S(2)}, u32[]{:S(2)}) collective-permute-start(f32[16,128,128]{2,1,0:T(8,128)} %get-tuple-element.30), channel_id=1, source_target_pairs={{0,32},{16,48},{32,0},{48,16},{64,96},{80,112},{96,64},{112,80},{1... | collective-permute-start | bytes 3145736 | tf_op jit(solution)/shard_map/ppermute | solution.py:16
  53.7 25.7 %collective-permute-start.2 = (f32[16,128,128]{2,1,0:T(8,128)}, f32[16,128,128]{2,1,0:T(8,128)}, u32[]{:S(2)}, u32[]{:S(2)}) collective-permute-start(f32[16,128,128]{2,1,0:T(8,128)} %get-tuple-element.32), channel_id=1, source_target_pairs={{0,64},{16,80},{32,96},{48,112},{64,0},{80,16},{96,32},{112,48},{1... | collective-permute-start | bytes 3145736 | tf_op jit(solution)/shard_map/ppermute | solution.py:16
  56.8 3.2 copy-start.2
  59.2 9.0 %copy-start.4 = (bf16[64,8,16,128]{3,2,1,0:T(8,128)(2,1)}, bf16[64,8,16,128]{3,2,1,0:T(8,128)(2,1)S(1)}, u32[]{:S(2)}) copy-start(bf16[64,8,16,128]{3,2,1,0:T(8,128)(2,1)S(1)} %copy.127) | copy-start | bytes 6291460
  93.2 1.3 copy-start.7
  106.7 7.3 %copy-start.10 = (bf16[1,512,2048]{1,2,0:T(8,128)(2,1)S(1)}, bf16[1,512,2048]{1,2,0:T(8,128)(2,1)}, u32[]{:S(2)}) copy-start(bf16[1,512,2048]{1,2,0:T(8,128)(2,1)} %copy.124) | copy-start | bytes 6291460
  106.7 7.3 %copy-start.11 = (bf16[512,16,128]{0,2,1:T(8,128)(2,1)S(1)}, bf16[512,16,128]{0,2,1:T(8,128)(2,1)}, u32[]{:S(2)}) copy-start(bf16[512,16,128]{0,2,1:T(8,128)(2,1)} %copy.95) | copy-start | bytes 6291460
  132.0 3.2 %copy-start.9 = (bf16[16,512,512]{1,2,0:T(8,128)(2,1)}, bf16[16,512,512]{1,2,0:T(8,128)(2,1)S(1)}, u32[]{:S(2)}) copy-start(bf16[16,512,512]{1,2,0:T(8,128)(2,1)S(1)} %get-tuple-element.27) | copy-start | bytes 25165828
  143.4 1.6 copy-start.5
  143.4 146.5 %reduce-scatter.3.cloned.1.call-start = ((), (), s32[]{:S(2)}) async-start(), calls=%async_computation.4 | async-start | bytes 9437184 | tf_op jit(solution)/shard_map/reduce_scatter | solution.py:139
  145.4 1.6 copy-start.8
  171.0 3.3 %copy-start.14 = (f32[512,512]{0,1:T(8,128)S(1)}, f32[512,512]{0,1:T(8,128)}, u32[]{:S(2)}) copy-start(f32[512,512]{0,1:T(8,128)} %constant.9.clone) | copy-start | bytes 3145732
  171.0 3.3 %copy-start.15 = (f32[512,512]{0,1:T(8,128)S(1)}, f32[512,512]{0,1:T(8,128)}, u32[]{:S(2)}) copy-start(f32[512,512]{0,1:T(8,128)} %constant.8.clone) | copy-start | bytes 3145732
  171.0 3.3 %copy-start.16 = (f32[512,512]{0,1:T(8,128)S(1)}, f32[512,512]{0,1:T(8,128)}, u32[]{:S(2)}) copy-start(f32[512,512]{0,1:T(8,128)} %constant.7.clone) | copy-start | bytes 3145732
  171.1 3.3 %copy-start.17 = (f32[512,512]{0,1:T(8,128)S(1)}, f32[512,512]{0,1:T(8,128)}, u32[]{:S(2)}) copy-start(f32[512,512]{0,1:T(8,128)} %constant.6.clone) | copy-start | bytes 3145732
  174.3 10.7 %copy-start.3 = (bf16[64,8,16,128]{3,2,1,0:T(8,128)(2,1)S(1)}, bf16[64,8,16,128]{3,2,1,0:T(8,128)(2,1)}, u32[]{:S(2)}) copy-start(bf16[64,8,16,128]{3,2,1,0:T(8,128)(2,1)} %copy.125) | copy-start | bytes 6291460
  185.0 5.4 %copy-start.13 = (f32[512,16,128]{2,0,1:T(8,128)S(1)}, f32[512,16,128]{2,0,1:T(8,128)}, u32[]{:S(2)}) copy-start(f32[512,16,128]{2,0,1:T(8,128)} %copy.84) | copy-start | bytes 12582916
  185.0 5.4 %copy-start.18 = (bf16[1,16,128,128]{3,2,1,0:T(8,128)(2,1)S(1)}, bf16[1,16,128,128]{3,2,1,0:T(8,128)(2,1)}, u32[]{:S(2)}) copy-start(bf16[1,16,128,128]{3,2,1,0:T(8,128)(2,1)} %fusion.36) | copy-start | bytes 1572868
  185.0 5.4 %copy-start.19 = (bf16[1,16,128,128]{3,2,1,0:T(8,128)(2,1)S(1)}, bf16[1,16,128,128]{3,2,1,0:T(8,128)(2,1)}, u32[]{:S(2)}) copy-start(bf16[1,16,128,128]{3,2,1,0:T(8,128)(2,1)} %get-tuple-element.29) | copy-start | bytes 1572868
  185.0 5.4 %copy-start.20 = (bf16[1,16,128,128]{3,2,1,0:T(8,128)(2,1)S(1)}, bf16[1,16,128,128]{3,2,1,0:T(8,128)(2,1)}, u32[]{:S(2)}) copy-start(bf16[1,16,128,128]{3,2,1,0:T(8,128)(2,1)} %get-tuple-element.31) | copy-start | bytes 1572868
  235.3 72.6 %all-to-all-start = ((f32[16,16,2048]{2,1,0:T(8,128)}), f32[16,16,2048]{2,1,0:T(8,128)}, u32[]{:S(2)}, u32[]{:S(2)}) async-start(f32[16,16,2048]{2,1,0:T(8,128)} %bitcast.144), calls=%async_computation.2 | async-start | bytes 4194304 | tf_op jit(solution)/shard_map/all_to_all | solution.py:26
  242.1 8.9 %copy-start.6 = (bf16[64,8,16,128]{3,2,1,0:T(8,128)(2,1)S(1)}, bf16[64,8,16,128]{3,2,1,0:T(8,128)(2,1)}, u32[]{:S(2)}) copy-start(bf16[64,8,16,128]{3,2,1,0:T(8,128)(2,1)} %copy-done.4) | copy-start | bytes 6291460
  295.0 4.0 %copy-start.12 = (f32[1,16,128,128]{3,2,1,0:T(8,128)S(1)}, f32[1,16,128,128]{3,2,1,0:T(8,128)}, u32[]{:S(2)}) copy-start(f32[1,16,128,128]{3,2,1,0:T(8,128)} %reduce-scatter.3.cloned.1.call-done) | copy-start | bytes 3145732
  299.0 11.3 %copy-start.1 = (bf16[1,512,2048]{2,1,0:T(8,128)(2,1)S(1)}, bf16[1,512,2048]{2,1,0:T(8,128)(2,1)}, u32[]{:S(2)}) copy-start(bf16[1,512,2048]{2,1,0:T(8,128)(2,1)} %param.15) | copy-start | bytes 6291460
Sparse Core Ops, SparseCore 0:
  10.2 73.8 all-gather.1
  143.5 91.7 reduce-scatter.4
  237.7 52.1 reduce-scatter.2
where the time goes:
time: 323 us; the launch traced here: 317 us
  matrix products  108 us (33%)
  waiting for transfers between devices  105 us (33%)
  local copies, waits for them, and re-layouts  53.6 us (17%)
  other arithmetic  22.8 us (7%)
  between operations  14.3 us (4%)
  starting transfers between devices  13.2 us (4%)
    ppermute x3, waiting for transfers between devices, swapped(): return lax.ppermute(value, axis, pairs)  36.9 us
    reduce_scatter x1, waiting for transfers between devices, local(): lax.psum_scatter(lax.dot_general(attn, grad_rows, (((0,), (0,)), ((), ())...  34.6 us
    reduce_scatter x1, waiting for transfers between devices, local(): lax.psum_scatter(jnp.einsum('nb,bhde->nhde', weights, far_grad, precision...  30.4 us
    unnamed x52, local copies, waits for them, and re-layouts  24.2 us
    dot_general x1, matrix products, local(): jnp.einsum('thd,shd->hts', grad_heads, value_heads, preferred_element_typ...  18 us
    reduce_sum x1, other arithmetic, local(): jnp.sum(energy * sel_mat[None], axis=2)  9.22 us
    dot_general x1, matrix products, local(): jnp.einsum('hts,thd->shd', probs, grad_heads, preferred_element_type=jnp....  8.93 us
    dot_general x1, matrix products, local(): lax.dot_general(grad_rows, lax.all_gather(out_weight, 'batch', axis=0, ti...  8.59 us
  transfers between devices with their start and end apart: 7, of which 6 were waited for; matrix products, arithmetic and copies ran while one was open for 38% of the time, Pallas kernels for 0%

commit v1 on v0

v1 whole, which is shorter than its diff:
```python
import jax
import jax.numpy as jnp
from jax import lax
from jax.experimental import pallas as pl
from jax.experimental.pallas import tpu as pltpu
from jax.sharding import PartitionSpec as P

H = 16
HD = 128
T = 512
D = 2048
HALF = 1024
SCALE = HD**-0.5
BF = jnp.bfloat16
F32 = jnp.float32
MESH = pl.DeviceIdType.MESH
COLS = ((0, 384), (384, 384), (768, 256))
ORDERS = ((1, 2, 0), (2, 0, 1), (0, 1, 2))


def dot(a, b, ca, cb):
    return lax.dot_general(a, b, (((ca,), (cb,)), ((), ())), preferred_element_type=F32)


def rem(a, b):
    return lax.rem(a, jnp.int32(b))


def div(a, b):
    return lax.div(a, jnp.int32(b))


def flip(a):
    return a + 1 - 2 * rem(a, 2)


def recv_shapes():
    shapes = []
    for piece, (_, width) in enumerate(COLS):
        dims = [4, 4, 4]
        for axis in ORDERS[piece]:
            for left in (2, 1):
                dims[axis] = left
                shapes.append(tuple(dims) + (2, 16, width))
    return shapes


def kernel(
    q_in, k_in, v_in, gain_in, w_in, d_in,
    dq_out, dk_out, dv_out, gain_out, wg_out,
    q_v, k_v, v_v, d_v, gain_v, w_g, attn, dosib, wq, probs, g_v, far,
    st, st_send, st_sib, cs_send, r1, run_send, r2,
    gt, sg0, recv12, cs12, r1b, r2b, r3b, sgsum, tacc, wgout, finsend,
    acc0, acc1, acc2,
    *rest,
):
    recvs = [rest[0:6], rest[6:12], rest[12:18]]
    lsem, ssem, rsem, asem, arsem = rest[18:]
    accs = (acc0, acc1, acc2)
    seq = lax.axis_index("seq")
    bat = lax.axis_index("batch")
    core, z = rem(seq, 2), div(seq, 2)
    x, y = div(bat, 4), rem(bat, 4)
    sib = (z * 2 + 1 - core, bat)

    def load(i, src, dst):
        return pltpu.make_async_copy(src, dst, lsem.at[i])

    loads = [
        load(0, k_in.at[0], k_v),
        load(1, v_in.at[0], v_v),
        load(2, q_in.at[0], q_v),
        load(3, gain_in.at[0], gain_v),
        load(4, d_in.at[0], d_v),
    ]
    for c in loads:
        c.start()

    a1 = x * (1 - core) + y * core
    a2 = y * (1 - core) + x * core
    wloads, wsteps = [], []
    for p in (0, 1):
        b1, b2 = rem(a1 + p, 4), rem(a2 + p, 4)

        def dev(c1, c2, p=p):
            o1, o2 = rem(c1 + 4 - p, 4), rem(c2 + 4 - p, 4)
            return (seq, (o1 * 4 + o2) * (1 - core) + (o2 * 4 + o1) * core)

        own = w_in.at[pl.ds(pl.multiple_of(core * 64 + p * 32, 32), 32), :]
        wloads.append(load(5 + p, own, w_g.at[core, p, b1, b2]))
        pair1, pair2 = div(b1, 2) * 2, div(b2, 2) * 2
        base = 10 * p
        steps = []

        def add(src, dst, device, base=base, steps=steps):
            i = base + len(steps)
            steps.append(
                pltpu.make_async_remote_copy(
                    src_ref=src, dst_ref=dst, send_sem=ssem.at[i], recv_sem=rsem.at[i],
                    device_id=device, device_id_type=MESH,
                )
            )

        one = w_g.at[core, p, b1, b2]
        add(own, one, dev(flip(b1), b2))
        two = w_g.at[core, p, pl.ds(pair1, 2), b2]
        add(two, two, dev(3 - b1, b2))
        four = w_g.at[core, p, :, b2]
        add(four, four, dev(b1, flip(b2)))
        eight = w_g.at[core, p, :, pl.ds(pair2, 2)]
        add(eight, eight, dev(b1, 3 - b2))
        add(four, four, sib)
        four2 = w_g.at[core, p, :, flip(b2)]
        add(four2, four2, sib)
        eight2 = w_g.at[core, p, :, pl.ds(2 - pair2, 2)]
        add(eight2, eight2, sib)
        wsteps.append(steps)
    for c in wloads:
        c.start()

    barrier = pltpu.get_barrier_semaphore()
    neighbours = [
        sib,
        (seq, flip(x) * 4 + y), (seq, (3 - x) * 4 + y),
        (seq, x * 4 + flip(y)), (seq, x * 4 + 3 - y),
        (flip(z) * 2 + core, bat), ((3 - z) * 2 + core, bat),
    ]
    for n in neighbours:
        pl.semaphore_signal(barrier, inc=1, device_id=n, device_id_type=MESH)
    pl.semaphore_wait(barrier, len(neighbours))

    def remote(i, src, dst, device):
        return pltpu.make_async_remote_copy(
            src_ref=src, dst_ref=dst, send_sem=ssem.at[i], recv_sem=rsem.at[i],
            device_id=device, device_id_type=MESH,
        )

    sent = []

    def start(c):
        c.start()
        sent.append(c)

    for p in (0, 1):
        start(wsteps[p][0])

    dcopy = remote(
        20, d_in.at[0, :, pl.ds(pl.multiple_of((1 - core) * HALF, HALF), HALF)], dosib, sib
    )
    start(dcopy)

    zp1 = (flip(z) * 2 + core, bat)
    zp3 = ((3 - z) * 2 + core, bat)
    mine = pl.ds(core * 8, 8)
    theirs = pl.ds((1 - core) * 8, 8)
    e0 = remote(21, st_send, st_sib, sib)
    e1 = remote(22, cs_send, r1, zp1)
    e2 = remote(23, run_send, r2, zp3)
    f1 = far.at[mine, pl.ds(128, 128)]
    f2 = far.at[mine, pl.ds(256, 128)]
    e1s = remote(24, f1, f1, sib)
    e2s = remote(25, f2, f2, sib)
    c0 = remote(26, gt.at[0], sg0, sib)
    c12 = remote(27, gt.at[pl.ds(1, 2), theirs], recv12, sib)
    c1 = remote(28, cs12.at[0], r1b, zp1)
    c2 = remote(29, cs12.at[1], r2b, zp3)
    c3 = remote(30, r2b, r3b, zp1)
    c4 = remote(31, sgsum.at[mine], sgsum.at[mine], sib)
    bit = [rem(seq, 2).astype(F32), rem(z, 2).astype(F32), div(z, 2).astype(F32)]

    rot = [rem(z + core, 4), rem(x + core, 4), rem(y + core, 4)]

    def axis_dev(axis, r):
        o = rem(r + 4 - core, 4)
        if axis == 0:
            return (o * 2 + core, bat)
        if axis == 1:
            return (seq, o * 4 + y)
        return (seq, x * 4 + o)

    rs_copies, rs_keeps = [], []
    for piece in range(3):
        copies, keeps = [], []
        cur = [pl.ds(0, 4)] * 3
        for axis in ORDERS[piece]:
            a = rot[axis]
            for sub in (0, 1):
                give, keep = list(cur), list(cur)
                if sub == 0:
                    give[axis] = pl.ds(2 - 2 * div(a, 2), 2)
                    keep[axis] = pl.ds(2 * div(a, 2), 2)
                    to = axis_dev(axis, 3 - a)
                else:
                    give[axis] = pl.ds(flip(a), 1)
                    keep[axis] = pl.ds(a, 1)
                    to = axis_dev(axis, flip(a))
                n = len(copies)
                copies.append(
                    remote(32 + piece * 6 + n, accs[piece].at[tuple(give)], recvs[piece][n], to)
                )
                keeps.append(tuple(keep))
                cur = keep
        rs_copies.append(copies)
        rs_keeps.append(keeps)

    def rs_start(n):
        for piece in range(3):
            start(rs_copies[piece][n])

    def rs_add(n):
        for piece in range(3):
            rs_copies[piece][n].wait_recv()
            keep, recv, acc = rs_keeps[piece][n], recvs[piece][n], accs[piece]
            lead = keep[0]

            def body(i, _, keep=keep, recv=recv, acc=acc, lead=lead):
                at = (lead.start + i,) + keep[1:]
                acc[at] = (acc[at].astype(F32) + recv[i].astype(F32)).astype(BF)
                return 0

            lax.fori_loop(0, lead.size, body, 0)

    def hcols(h):
        return pl.ds(pl.multiple_of(h * HD, HD), HD)

    def rolled(h):
        return pltpu.roll(gain_v[...], rem(jnp.int32(HD) - h, HD), 1)

    loads[0].wait()
    loads[1].wait()

    def state_body(h, _):
        kh, vh = k_v[:, hcols(h)], v_v[:, hcols(h)]
        lo = dot(kh[:256], vh[:256], 0, 0)
        both = lo + dot(kh[256:], vh[256:], 0, 0)
        far[h, 384:512] = lo.astype(BF)
        st[h] = both
        st_send[h] = both.astype(BF)
        return 0

    lax.fori_loop(0, H, state_body, 0)
    start(e0)
    for p in (0, 1):
        wloads[p].wait()
        wsteps[p][0].wait_recv()
        start(wsteps[p][1])
    loads[2].wait()
    loads[3].wait()

    rr = lax.broadcasted_iota(jnp.int32, (128, 128), 0)
    cc = lax.broadcasted_iota(jnp.int32, (128, 128), 1)
    same = (rr < 64) == (cc < 64)
    m0 = (rr >= cc) & same
    m1 = (rr >= 64) & (cc < 64)

    def diag_mask(w0, w1):
        return jnp.where(m0, w0, jnp.where(m1, w1, 0.0))

    def ev_e0():
        e0.wait_recv()

        def body(h, _):
            far[h, 0:128] = (st_sib[h].astype(F32) * bit[0]).astype(BF)
            return 0

        lax.fori_loop(0, H, body, 0)

        def body2(i, _):
            total = st[core * 8 + i] + st_sib[core * 8 + i].astype(F32)
            st[core * 8 + i] = total
            cs_send[i] = total.astype(BF)
            return 0

        lax.fori_loop(0, 8, body2, 0)
        start(e1)

    def ev_e1():
        e1.wait_recv()

        def body(i, _):
            got = r1[i].astype(F32)
            far[core * 8 + i, 128:256] = (got * bit[1]).astype(BF)
            run_send[i] = (st[core * 8 + i] + got).astype(BF)
            return 0

        lax.fori_loop(0, 8, body, 0)
        start(e2)
        start(e1s)

    def ev_e2():
        e2.wait_recv()

        def body(i, _):
            far[core * 8 + i, 256:384] = (r2[i].astype(F32) * bit[2]).astype(BF)
            return 0

        lax.fori_loop(0, 8, body, 0)
        start(e2s)

    def ev_w2():
        for p in (0, 1):
            wsteps[p][1].wait_recv()
            start(wsteps[p][2])
            start(wsteps[p][4])

    def ev_w3():
        for p in (0, 1):
            wsteps[p][2].wait_recv()
            start(wsteps[p][3])
            start(wsteps[p][5])

    def ev_w4():
        for p in (0, 1):
            wsteps[p][3].wait_recv()
            start(wsteps[p][6])

    def probs_body(h, _):
        wr = rolled(h) * SCALE
        ws = [wr[:, 16 * l : 16 * l + 1] for l in range(7)]
        qh, kh = q_v[:, hcols(h)], k_v[:, hcols(h)]
        for blk in (0, 1):
            r0 = 256 * blk
            sc = dot(qh[r0 : r0 + 256], kh[r0 : r0 + 256], 1, 1)
            a, b = slice(r0, r0 + 128), slice(r0 + 128, r0 + 256)
            probs[h, blk, 0:128, 0:128] = (sc[:128, :128] * diag_mask(ws[0][a], ws[1][a])).astype(BF)
            probs[h, blk, 0:128, 128:256] = jnp.zeros((128, 128), BF)
            probs[h, blk, 128:256, 0:128] = (sc[128:, :128] * ws[2][b]).astype(BF)
            probs[h, blk, 128:256, 128:256] = (
                sc[128:, 128:] * diag_mask(ws[0][b], ws[1][b])
            ).astype(BF)
        qf = qh.astype(F32)
        for b in range(3):
            wq[h, :, 128 * b : 128 * b + 128] = (qf * ws[4 + b]).astype(BF)
        wq[h, 0:256, 384:512] = jnp.zeros((256, 128), BF)
        wq[h, 256:512, 384:512] = (qf[256:] * ws[3][256:]).astype(BF)
        return 0

    def run(body, cuts):
        at = 0
        for stop, event in cuts:
            if stop > at:
                lax.fori_loop(at, stop, body, 0)
            at = stop
            if event is not None:
                event()

    run(probs_body, [(3, ev_e0), (5, ev_w2), (11, ev_e1), (13, ev_w3), (16, None)])
    ev_e2()
    e1s.wait_recv()
    e2s.wait_recv()

    def attn_copy(h):
        return pltpu.make_async_remote_copy(
            src_ref=attn.at[0, h], dst_ref=attn.at[1, h], send_sem=asem.at[h],
            recv_sem=arsem.at[h], device_id=sib, device_id_type=MESH,
        )

    def attn_body(h, _):
        vh = v_v[:, hcols(h)]
        cross = dot(wq[h], far[h], 1, 0)
        for blk in (0, 1):
            r0 = 256 * blk
            out = dot(probs[h, blk], vh[r0 : r0 + 256], 1, 0) + cross[r0 : r0 + 256]
            attn[0, h, r0 : r0 + 256] = out.astype(BF)
        attn_copy(h).start()
        return 0

    lax.fori_loop(0, H, attn_body, 0)

    loads[4].wait()
    dcopy.wait_recv()

    def wg_body(h, _):
        attn_copy(h).wait_recv()
        own = d_v[:, pl.ds(pl.multiple_of(core * HALF, HALF), HALF)]
        part = dot(attn[0, h], own, 0, 0) + dot(attn[1, h], dosib[...], 0, 0)
        part = part.astype(BF)
        zd = rem(div(h, 4) + core, 4)
        cd = rem(div(h, 2), 2)
        for xi in (0, 1):
            xd = rem(2 * rem(h, 2) + xi + core, 4)
            for yi in range(4):
                yd = rem(yi + core, 4)
                row = (xi * 4 + yi) * 16
                for piece, (c0_, width) in enumerate(COLS):
                    accs[piece][zd, xd, yd, cd] = part[row : row + 16, c0_ : c0_ + width]
        return 0

    lax.fori_loop(0, H, wg_body, 0)
    rs_start(0)

    ev_w4()
    for p in (0, 1):
        for i in (4, 5, 6):
            wsteps[p][i].wait_recv()

    def g_body(i, _):
        blocks = []
        for j in (0, 1):
            h = 2 * i + j
            hx, hy = div(h, 4), rem(h, 4)
            hx1, hy1 = rem(hx + 1, 4), rem(hy + 1, 4)
            blocks += [w_g[0, 0, hx, hy], w_g[0, 1, hx1, hy1], w_g[1, 0, hy, hx], w_g[1, 1, hy1, hx1]]
        weight = jnp.concatenate(blocks, axis=0)
        out = dot(d_v[...], weight, 1, 1).astype(BF)
        for j in (0, 1):
            h = 2 * i + j
            gh = out[:, 128 * j : 128 * j + 128]
            g_v[h] = gh
            grads = dot(gh, wq[h], 0, 0)
            for b in range(3):
                gt[b, h] = (grads[:, 128 * b : 128 * b + 128] * bit[b]).astype(BF)
            gt[3, h] = grads[:, 384:512].astype(BF)
        return 0

    lax.fori_loop(0, H // 2, g_body, 0)
    start(c0)
    start(c12)

    def ev_c12():
        c12.wait_recv()

        def body(i, _):
            for b in (0, 1):
                cs12[b, i] = (gt[1 + b, core * 8 + i].astype(F32) + recv12[b, i].astype(F32)).astype(BF)
            return 0

        lax.fori_loop(0, 8, body, 0)
        start(c1)
        start(c2)

    def ev_c2():
        c2.wait_recv()
        start(c3)

    def ev_c3():
        c1.wait_recv()
        c3.wait_recv()

        def body(i, _):
            total = r1b[i].astype(F32) + r2b[i].astype(F32) + r3b[i].astype(F32)
            sgsum[core * 8 + i] = total.astype(BF)
            return 0

        lax.fori_loop(0, 8, body, 0)
        start(c4)

    def ev_rs(n):
        def event():
            rs_add(n)
            rs_start(n + 1)

        return event

    def wait_attn(h, _):
        attn_copy(h).wait_send()
        return 0

    lax.fori_loop(0, H, wait_attn, 0)
    tacc[...] = jnp.zeros_like(tacc)
    dsel = lax.broadcasted_iota(jnp.int32, (256, 128), 1) - 16 * div(
        lax.broadcasted_iota(jnp.int32, (256, 128), 0), 64
    )
    frow = lax.broadcasted_iota(jnp.int32, (512, 128), 0)
    dfar = lax.broadcasted_iota(jnp.int32, (512, 128), 1) - 64 - 16 * div(frow, 128)

    def dq_body(h, _):
        wr = rolled(h) * SCALE
        ws = [wr[:, 16 * l : 16 * l + 1] for l in range(7)]
        qf = q_v[:, hcols(h)].astype(F32)
        kh, vh, gh = k_v[:, hcols(h)], v_v[:, hcols(h)], g_v[h]
        sel = (dsel == h).astype(F32).astype(BF)
        fsel = (dfar == h).astype(F32).astype(BF)
        dq = None
        prods = []
        for b in range(3):
            pb = dot(gh, far[h, 128 * b : 128 * b + 128], 1, 1)
            prods.append((qf * pb).astype(BF))
            term = pb * ws[4 + b]
            dq = term if dq is None else dq + term
        p3 = dot(gh[256:], far[h, 384:512], 1, 1)
        prod3 = (qf[256:] * p3).astype(BF)
        p3 = p3 * ws[3][256:]
        for blk in (0, 1):
            r0 = 256 * blk
            pg = dot(gh[r0 : r0 + 256], vh[r0 : r0 + 256], 1, 1)
            a, b = slice(r0, r0 + 128), slice(r0 + 128, r0 + 256)
            top = jnp.concatenate(
                [(pg[:128, :128] * diag_mask(ws[0][a], ws[1][a])).astype(BF), jnp.zeros((128, 128), BF)], axis=1
            )
            bottom = jnp.concatenate(
                [
                    (pg[128:, :128] * ws[2][b]).astype(BF),
                    (pg[128:, 128:] * diag_mask(ws[0][b], ws[1][b])).astype(BF),
                ],
                axis=1,
            )
            sg = jnp.concatenate([top, bottom], axis=0)
            wq[h, r0 : r0 + 256, 0:256] = sg
            energy = (pg * probs[h, blk].astype(F32)).astype(BF)
            out = dot(sg, kh[r0 : r0 + 256], 1, 0) + dq[r0 : r0 + 256]
            fars = [prods[b][r0 : r0 + 256] for b in range(3)]
            if blk == 1:
                out = out + p3
                fars.append(prod3)
                sums = dot(jnp.concatenate(fars, axis=1), fsel, 1, 0)
            else:
                sums = dot(jnp.concatenate(fars, axis=1), fsel[:384], 1, 0)
            attn[0, h, r0 : r0 + 256] = out.astype(BF)
            tacc[r0 : r0 + 256] += sums + dot(energy, sel, 1, 0)
        pltpu.make_async_copy(attn.at[0, h], dq_out.at[0, :, hcols(h)], lsem.at[8 + h]).start()
        return 0

    run(
        dq_body,
        [(1, ev_c12), (6, ev_c2), (8, ev_rs(0)), (11, ev_rs(1)), (12, ev_c3), (14, ev_rs(2)), (15, ev_rs(3)), (16, None)],
    )
    c0.wait_recv()
    c4.wait_recv()

    def dk_body(h, _):
        base = sg0[h].astype(F32) + sgsum[h].astype(F32)
        halves = ((base + gt[3, h].astype(F32)).astype(BF), base.astype(BF))
        for blk in (0, 1):
            rows = pl.ds(256 * blk, 256)
            kb, vb, qb = k_v[rows, hcols(h)], v_v[rows, hcols(h)], q_v[rows, hcols(h)]
            gb = g_v[h, rows]
            dv = dot(probs[h, blk], gb, 0, 0) + dot(kb, halves[blk], 1, 1)
            dk = dot(wq[h, rows, 0:256], qb, 0, 0) + dot(vb, halves[blk], 1, 0)
            k_v[rows, hcols(h)] = dk.astype(BF)
            v_v[rows, hcols(h)] = dv.astype(BF)
        pltpu.make_async_copy(k_v.at[:, hcols(h)], dk_out.at[0, :, hcols(h)], lsem.at[24 + h]).start()
        pltpu.make_async_copy(v_v.at[:, hcols(h)], dv_out.at[0, :, hcols(h)], lsem.at[40 + h]).start()
        return 0

    run(dk_body, [(6, ev_rs(4)), (16, None)])

    lane = lax.broadcasted_iota(jnp.int32, (64, 128), 1)
    for i in range(8):
        rows = slice(64 * i, 64 * i + 64)
        g4 = i % 4
        t = tacc[rows]

        def moved(frm, to, t=t):
            shift = (to - frm) * 16 % 128
            return pltpu.roll(t, shift, 1) if shift else t

        res = jnp.where(lane < 16, moved(g4, 0), 0.0)
        if g4 % 2 == 1:
            res = jnp.where((lane >= 16) & (lane < 32), moved(g4 - 1, 1), res)
        if g4 >= 2:
            res = jnp.where((lane >= 32) & (lane < 48), moved(0, 2) + moved(1, 2), res)
        res = res / gain_v[rows]
        if i >= 4:
            res = jnp.where((lane >= 48) & (lane < 64), moved(7, 3) * SCALE, res)
        res = jnp.where((lane >= 64) & (lane < 112), t * SCALE, res)
        tacc[rows] = res
    gcopy = pltpu.make_async_copy(tacc, gain_out.at[0], lsem.at[56])
    gcopy.start()

    for piece, (c0_, width) in enumerate(COLS):
        rs_copies[piece][5].wait_recv()
        acc, recv = accs[piece], recvs[piece][5]
        own_at = (rot[0], rot[1], rot[2], core)
        sib_at = (rot[0], rot[1], rot[2], 1 - core)
        wgout[core, :, c0_ : c0_ + width] = acc[own_at].astype(F32) + recv[0, 0, 0, core].astype(F32)
        finsend[:, c0_ : c0_ + width] = acc[sib_at].astype(F32) + recv[0, 0, 0, 1 - core].astype(F32)
    last = remote(50, finsend, wgout.at[core], sib)
    start(last)
    last.wait_recv()
    outs = [
        pltpu.make_async_copy(wgout.at[i], wg_out.at[:, pl.ds(HALF * i, HALF)], lsem.at[57 + i])
        for i in (0, 1)
    ]
    for c in outs:
        c.start()
    for c in sent:
        c.wait_send()

    def wait_out(h, _):
        pltpu.make_async_copy(attn.at[0, h], dq_out.at[0, :, hcols(h)], lsem.at[8 + h]).wait()
        pltpu.make_async_copy(k_v.at[:, hcols(h)], dk_out.at[0, :, hcols(h)], lsem.at[24 + h]).wait()
        pltpu.make_async_copy(v_v.at[:, hcols(h)], dv_out.at[0, :, hcols(h)], lsem.at[40 + h]).wait()
        return 0

    lax.fori_loop(0, H, wait_out, 0)
    gcopy.wait()
    for c in outs:
        c.wait()


def local(queries, keys, values, level_gain, out_weight, out_grad):
    big = jax.ShapeDtypeStruct((1, T, D), BF)
    scratch = [
        pltpu.VMEM((T, D), BF),
        pltpu.VMEM((T, D), BF),
        pltpu.VMEM((T, D), BF),
        pltpu.VMEM((T, D), BF),
        pltpu.VMEM((T, HD), F32),
        pltpu.VMEM((2, 2, 4, 4, 32, D), BF),
        pltpu.VMEM((2, H, T, HD), BF),
        pltpu.VMEM((T, HALF), BF),
        pltpu.VMEM((H, T, T), BF),
        pltpu.VMEM((H, 2, 256, 256), BF),
        pltpu.VMEM((H, T, HD), BF),
        pltpu.VMEM((H, T, HD), BF),
        pltpu.VMEM((H, HD, HD), F32),
        pltpu.VMEM((H, HD, HD), BF),
        pltpu.VMEM((H, HD, HD), BF),
        pltpu.VMEM((8, HD, HD), BF),
        pltpu.VMEM((8, HD, HD), BF),
        pltpu.VMEM((8, HD, HD), BF),
        pltpu.VMEM((8, HD, HD), BF),
        pltpu.VMEM((4, H, HD, HD), BF),
        pltpu.VMEM((H, HD, HD), BF),
        pltpu.VMEM((2, 8, HD, HD), BF),
        pltpu.VMEM((2, 8, HD, HD), BF),
        pltpu.VMEM((8, HD, HD), BF),
        pltpu.VMEM((8, HD, HD), BF),
        pltpu.VMEM((8, HD, HD), BF),
        pltpu.VMEM((H, HD, HD), BF),
        pltpu.VMEM((T, HD), F32),
        pltpu.VMEM((2, 16, HALF), F32),
        pltpu.VMEM((16, HALF), F32),
    ]
    scratch += [pltpu.VMEM((4, 4, 4, 2, 16, width), BF) for _, width in COLS]
    scratch += [pltpu.VMEM(shape, BF) for shape in recv_shapes()]
    scratch += [
        pltpu.SemaphoreType.DMA((60,)),
        pltpu.SemaphoreType.DMA((52,)),
        pltpu.SemaphoreType.DMA((52,)),
        pltpu.SemaphoreType.DMA((H,)),
        pltpu.SemaphoreType.DMA((H,)),
    ]
    anyspace = pl.BlockSpec(memory_space=pl.ANY)
    return pl.pallas_call(
        kernel,
        out_shape=(
            big, big, big,
            jax.ShapeDtypeStruct((1, T, HD), F32),
            jax.ShapeDtypeStruct((16, D), F32),
        ),
        in_specs=[anyspace] * 6,
        out_specs=(anyspace,) * 5,
        scratch_shapes=scratch,
        compiler_params=pltpu.CompilerParams(
            collective_id=0, has_side_effects=True, vmem_limit_bytes=62 * 2**20
        ),
        cost_estimate=pl.CostEstimate(flops=20 * 10**9, bytes_accessed=16 * 2**20, transcendentals=0),
    )(queries, keys, values, level_gain, out_weight, out_grad)


def solution(mesh):
    tokens = P("batch", "seq", None)
    return jax.shard_map(
        local,
        mesh=mesh,
        in_specs=(tokens, tokens, tokens, tokens, P("batch", None), tokens),
        out_specs=(tokens, tokens, tokens, tokens, P(("seq", "batch"), None)),
        check_vma=False,
    )
```

time: 323 us -> 109 us (0.34); the launches traced: 317 us -> 109 us
  matrix products: 108 us -> 0 us
  waiting for transfers between devices: 105 us -> 0 us
  Pallas kernels: 0 us -> 99.8 us
  local copies, waits for them, and re-layouts: 53.6 us -> 8.34 us
  other arithmetic: 22.8 us -> 0 us
  between operations: 14.3 us -> 0.65 us
  starting transfers between devices: 13.2 us -> 0 us
    dot_general x15 -> x0, matrix products: 108 us -> none  [the longest x1 18 us: local(): jnp.einsum('thd,shd->hts', grad_heads, value_heads, preferred_element_typ...]
    pallas_call x0 -> x1, Pallas kernels: none -> 99.8 us  [local(): pl.pallas_call(kernel, out_shape=(big, big, big, jax.ShapeDtypeStruct((1,...]
    reduce_scatter x2 -> x0, waiting for transfers between devices: 65 us -> none  [the longest x1 34.6 us: local(): lax.psum_scatter(lax.dot_general(attn, grad_rows, (((0,), (0,)), ((), ())...]
    ppermute x3 -> x0, waiting for transfers between devices: 36.9 us -> none  [swapped(): return lax.ppermute(value, axis, pairs)]
    unnamed x52 -> x13, local copies, waits for them, and re-layouts: 24.2 us -> 8.34 us
    reduce_sum x2 -> x0, other arithmetic: 11.6 us -> none  [the longest x1 9.22 us: local(): jnp.sum(energy * sel_mat[None], axis=2)]
    mul x3 -> x0, local copies, waits for them, and re-layouts: 10.4 us -> none  [the longest x1 5.35 us: local(): projected * grad_heads[None]]
    another operation x3 -> x0, other arithmetic: 7.7 us -> none  [local(): far_stack = jnp.stack(far_list)]
  transfers between devices with their start and end apart: 7 -> 0, of which waited for: 6 -> 0; matrix products, arithmetic and copies ran while one was open for 38% -> 0% of each run, Pallas kernels for 0% -> 0%
where the time goes in v1:
time: 109 us
  Pallas kernels  99.8 us (92%)
  local copies, waits for them, and re-layouts  8.34 us (8%)
    pallas_call x1, Pallas kernels, local(): pl.pallas_call(kernel, out_shape=(big, big, big, jax.ShapeDtypeStruct((1,...  99.8 us
    unnamed x13, local copies, waits for them, and re-layouts  8.34 us

profile of v1, /device:TPU:1, one launch (start us, length us, event | category | flops | bytes accessed | tf_op | source)
XLA Modules:
  0.0 108.8 jit_solution(13006000315405522651)
XLA Ops:
  0.6 99.8 %shard_map.101 = (bf16[1,512,2048]{2,1,0:T(8,128)(2,1)}, bf16[1,512,2048]{2,1,0:T(8,128)(2,1)}, bf16[1,512,2048]{2,1,0:T(8,128)(2,1)}, f32[1,512,128]{2,1,0:T(8,128)}, f32[16,2048]{1,0:T(8,128)}) custom-call(bf16[1,512,2048]{2,1,0:T(8,128)(2,1)} %q_in.1, bf16[1,512,2048]{2,1,0:T(8,128)(2,1)} %k_in.1, bf16[1,512,2048]{2,1,0:T(8,128)(2,1)} %v_in.1, ...), custom_call_target="tpu_custom_call" | custom-call | flops 20000000000 | bytes 16777216 | tf_op jit(solution)/shard_map/pallas_call | solution.py:636
  100.4 0.0 copy-start.1
  100.4 3.3 %copy.16 = bf16[1,512,2048]{2,1,0:T(8,128)(2,1)} copy(bf16[1,512,2048]{2,1,0:T(8,128)(2,1)} %get-tuple-element.10) | data formatting | bytes 4194304
  103.7 0.0 copy-done.1
  103.7 0.0 copy-start
  103.7 1.3 %copy.17 = bf16[1,512,2048]{2,1,0:T(8,128)(2,1)} copy(bf16[1,512,2048]{2,1,0:T(8,128)(2,1)S(1)} %copy-done.1) | data formatting | bytes 4194304
  105.1 1.0 copy-done
  106.1 0.0 copy-start.2
  106.1 0.0 copy-start.3
  106.1 1.3 %copy.18 = bf16[1,512,2048]{2,1,0:T(8,128)(2,1)} copy(bf16[1,512,2048]{2,1,0:T(8,128)(2,1)S(1)} %copy-done) | data formatting | bytes 4194304
  107.4 0.0 copy-done.2
  107.4 0.7 copy.19
  108.1 0.0 copy-done.3
  108.1 0.7 copy.20
Async XLA Ops:
  100.4 3.3 %copy-start.1 = (bf16[1,512,2048]{2,1,0:T(8,128)(2,1)S(1)}, bf16[1,512,2048]{2,1,0:T(8,128)(2,1)}, u32[]{:S(2)}) copy-start(bf16[1,512,2048]{2,1,0:T(8,128)(2,1)} %get-tuple-element.11) | copy-start | bytes 6291460
  103.7 2.3 %copy-start = (bf16[1,512,2048]{2,1,0:T(8,128)(2,1)S(1)}, bf16[1,512,2048]{2,1,0:T(8,128)(2,1)}, u32[]{:S(2)}) copy-start(bf16[1,512,2048]{2,1,0:T(8,128)(2,1)} %get-tuple-element.12) | copy-start | bytes 6291460
  106.1 1.3 %copy-start.2 = (f32[1,512,128]{2,1,0:T(8,128)S(1)}, f32[1,512,128]{2,1,0:T(8,128)}, u32[]{:S(2)}) copy-start(f32[1,512,128]{2,1,0:T(8,128)} %get-tuple-element.13) | copy-start | bytes 786436
  106.1 2.0 %copy-start.3 = (f32[16,2048]{1,0:T(8,128)S(1)}, f32[16,2048]{1,0:T(8,128)}, u32[]{:S(2)}) copy-start(f32[16,2048]{1,0:T(8,128)} %get-tuple-element.14) | copy-start | bytes 393220

commit v2 on v1

--- a/solution.py
+++ b/solution.py
@@ -48,15 +48,17 @@
 def kernel(
     q_in, k_in, v_in, gain_in, w_in, d_in,
     dq_out, dk_out, dv_out, gain_out, wg_out,
-    q_v, k_v, v_v, d_v, gain_v, w_g, attn, dosib, wq, probs, g_v, far,
-    st, st_send, st_sib, cs_send, r1, run_send, r2,
-    gt, sg0, recv12, cs12, r1b, r2b, r3b, sgsum, tacc, wgout, finsend,
-    acc0, acc1, acc2,
+    q_v, d_v, gain_v, w_g, attn_sib, dosib, wq, probs, g_v, far,
+    st, st_sib, total, cs_send, r1, run_send, r2,
+    gt, sg0, recv12, cs12, r1b, r2b, r3b, sgsum, wgout, finsend,
+    acc0, acc1, acc2, fk0, fk1, fk2,
     *rest,
 ):
     recvs = [rest[0:6], rest[6:12], rest[12:18]]
     lsem, ssem, rsem, asem, arsem = rest[18:]
     accs = (acc0, acc1, acc2)
+    kept = (fk0, fk1, fk2)
+    k_v, v_v, own_v, tacc = dk_out.at[0], dv_out.at[0], dq_out.at[0], gain_out.at[0]
     seq = lax.axis_index("seq")
     bat = lax.axis_index("batch")
     core, z = rem(seq, 2), div(seq, 2)
@@ -151,21 +153,22 @@
 
     zp1 = (flip(z) * 2 + core, bat)
     zp3 = ((3 - z) * 2 + core, bat)
-    mine = pl.ds(core * 8, 8)
-    theirs = pl.ds((1 - core) * 8, 8)
-    e0 = remote(21, st_send, st_sib, sib)
-    e1 = remote(22, cs_send, r1, zp1)
-    e2 = remote(23, run_send, r2, zp3)
-    f1 = far.at[mine, pl.ds(128, 128)]
-    f2 = far.at[mine, pl.ds(256, 128)]
-    e1s = remote(24, f1, f1, sib)
-    e2s = remote(25, f2, f2, sib)
-    c0 = remote(26, gt.at[0], sg0, sib)
-    c12 = remote(27, gt.at[pl.ds(1, 2), theirs], recv12, sib)
-    c1 = remote(28, cs12.at[0], r1b, zp1)
-    c2 = remote(29, cs12.at[1], r2b, zp3)
-    c3 = remote(30, r2b, r3b, zp1)
-    c4 = remote(31, sgsum.at[mine], sgsum.at[mine], sib)
+    e0, e1, e2, es, c0, c12, c1, c2, c3, c4 = [[] for _ in range(10)]
+    for j in (0, 1):
+        four = pl.ds(4 * j, 4)
+        n = 51 + 10 * j
+        e0.append(remote(n, st.at[:, four], st_sib.at[:, four], sib))
+        e1.append(remote(n + 1, cs_send.at[four], r1.at[four], zp1))
+        e2.append(remote(n + 2, run_send.at[four], r2.at[four], zp3))
+        fars = far.at[core, four, pl.ds(128, 256)]
+        es.append(remote(n + 3, fars, fars, sib))
+        c0.append(remote(n + 4, gt.at[0, :, four], sg0.at[:, four], sib))
+        c12.append(remote(n + 5, gt.at[pl.ds(1, 2), 1 - core, four], recv12.at[:, four], sib))
+        c1.append(remote(n + 6, cs12.at[0, four], r1b.at[four], zp1))
+        c2.append(remote(n + 7, cs12.at[1, four], r2b.at[four], zp3))
+        c3.append(remote(n + 8, r2b.at[four], r3b.at[four], zp1))
+        sums = sgsum.at[core, four]
+        c4.append(remote(n + 9, sums, sums, sib))
     bit = [rem(seq, 2).astype(F32), rem(z, 2).astype(F32), div(z, 2).astype(F32)]
 
     rot = [rem(z + core, 4), rem(x + core, 4), rem(y + core, 4)]
@@ -178,10 +181,11 @@
             return (seq, o * 4 + y)
         return (seq, x * 4 + o)
 
-    rs_copies, rs_keeps = [], []
+    rs_copies, rs_keeps, rs_kept = [], [], []
     for piece in range(3):
-        copies, keeps = [], []
+        copies, keeps, local_keeps = [], [], []
         cur = [pl.ds(0, 4)] * 3
+        cur_local = [pl.ds(0, 4)] * 3
         for axis in ORDERS[piece]:
             a = rot[axis]
             for sub in (0, 1):
@@ -200,8 +204,14 @@
                 )
                 keeps.append(tuple(keep))
                 cur = keep
+                if axis == ORDERS[piece][0]:
+                    cur_local[axis] = pl.ds(0, 2) if sub == 0 else pl.ds(rem(a, 2), 1)
+                else:
+                    cur_local[axis] = keep[axis]
+                local_keeps.append(tuple(cur_local))
         rs_copies.append(copies)
         rs_keeps.append(keeps)
+        rs_kept.append(local_keeps)
 
     def rs_start(n):
         for piece in range(3):
@@ -210,15 +220,19 @@
     def rs_add(n):
         for piece in range(3):
             rs_copies[piece][n].wait_recv()
-            keep, recv, acc = rs_keeps[piece][n], recvs[piece][n], accs[piece]
-            lead = keep[0]
-
-            def body(i, _, keep=keep, recv=recv, acc=acc, lead=lead):
-                at = (lead.start + i,) + keep[1:]
-                acc[at] = (acc[at].astype(F32) + recv[i].astype(F32)).astype(BF)
+            keep, local_keep = rs_keeps[piece][n], rs_kept[piece][n]
+            recv, acc, f32s = recvs[piece][n], accs[piece], kept[piece]
+
+            def body(i, _, keep=keep, local_keep=local_keep, recv=recv, acc=acc, f32s=f32s):
+                at = (keep[0].start + i,) + keep[1:]
+                local_at = (local_keep[0].start + i,) + local_keep[1:]
+                before = acc[at].astype(F32) if n == 0 else f32s[local_at]
+                value = before + recv[i].astype(F32)
+                f32s[local_at] = value
+                acc[at] = value.astype(BF)
                 return 0
 
-            lax.fori_loop(0, lead.size, body, 0)
+            lax.fori_loop(0, keep[0].size, body, 0)
 
     def hcols(h):
         return pl.ds(pl.multiple_of(h * HD, HD), HD)
@@ -229,21 +243,46 @@
     loads[0].wait()
     loads[1].wait()
 
-    def state_body(h, _):
+    def chunked(i):
+        j, r = div(i, 8), rem(i, 8)
+        return div(r, 4), 4 * j + rem(r, 4)
+
+    def head(i):
+        hi, lo = chunked(i)
+        return hi * 8 + lo
+
+    def state_body(i, _):
+        hi, lo = chunked(i)
+        h = hi * 8 + lo
         kh, vh = k_v[:, hcols(h)], v_v[:, hcols(h)]
-        lo = dot(kh[:256], vh[:256], 0, 0)
-        both = lo + dot(kh[256:], vh[256:], 0, 0)
-        far[h, 384:512] = lo.astype(BF)
-        st[h] = both
-        st_send[h] = both.astype(BF)
+        low = dot(kh[:256], vh[:256], 0, 0)
+        far[hi, lo, 384:512] = low.astype(BF)
+        st[hi, lo] = low + dot(kh[256:], vh[256:], 0, 0)
         return 0
 
-    lax.fori_loop(0, H, state_body, 0)
-    start(e0)
-    for p in (0, 1):
-        wloads[p].wait()
-        wsteps[p][0].wait_recv()
-        start(wsteps[p][1])
+    def ev_w1():
+        for p in (0, 1):
+            wloads[p].wait()
+            wsteps[p][0].wait_recv()
+            start(wsteps[p][1])
+
+    def run(body, cuts):
+        at = 0
+        for stop, *events in cuts:
+            if stop > at:
+                lax.fori_loop(at, stop, body, 0)
+            at = stop
+            for event in events:
+                event()
+
+    def starts(*copies):
+        def event():
+            for c in copies:
+                start(c)
+
+        return event
+
+    run(state_body, [(4, ev_w1), (8, starts(e0[0])), (16, starts(e0[1]))])
     loads[2].wait()
     loads[3].wait()
 
@@ -256,46 +295,56 @@
     def diag_mask(w0, w1):
         return jnp.where(m0, w0, jnp.where(m1, w1, 0.0))
 
-    def ev_e0():
-        e0.wait_recv()
-
-        def body(h, _):
-            far[h, 0:128] = (st_sib[h].astype(F32) * bit[0]).astype(BF)
-            return 0
-
-        lax.fori_loop(0, H, body, 0)
-
-        def body2(i, _):
-            total = st[core * 8 + i] + st_sib[core * 8 + i].astype(F32)
-            st[core * 8 + i] = total
-            cs_send[i] = total.astype(BF)
-            return 0
-
-        lax.fori_loop(0, 8, body2, 0)
-        start(e1)
-
-    def ev_e1():
-        e1.wait_recv()
-
-        def body(i, _):
-            got = r1[i].astype(F32)
-            far[core * 8 + i, 128:256] = (got * bit[1]).astype(BF)
-            run_send[i] = (st[core * 8 + i] + got).astype(BF)
-            return 0
-
-        lax.fori_loop(0, 8, body, 0)
-        start(e2)
-        start(e1s)
-
-    def ev_e2():
-        e2.wait_recv()
-
-        def body(i, _):
-            far[core * 8 + i, 256:384] = (r2[i].astype(F32) * bit[2]).astype(BF)
-            return 0
-
-        lax.fori_loop(0, 8, body, 0)
-        start(e2s)
+    def ev_e0(j):
+        def event():
+            e0[j].wait_recv()
+
+            def body(i, _):
+                m = 4 * j + i
+                for hi in (0, 1):
+                    far[hi, m, 0:128] = (st_sib[hi, m] * bit[0]).astype(BF)
+                chip = st[core, m] + st_sib[core, m]
+                total[m] = chip
+                cs_send[m] = chip.astype(BF)
+                return 0
+
+            lax.fori_loop(0, 4, body, 0)
+            start(e1[j])
+
+        return event
+
+    def ev_e1(j):
+        def event():
+            e1[j].wait_recv()
+
+            def body(i, _):
+                m = 4 * j + i
+                got = r1[m].astype(F32)
+                far[core, m, 128:256] = (got * bit[1]).astype(BF)
+                run_send[m] = (total[m] + got).astype(BF)
+                return 0
+
+            lax.fori_loop(0, 4, body, 0)
+            start(e2[j])
+
+        return event
+
+    def ev_e2(j):
+        def event():
+            e2[j].wait_recv()
+
+            def body(i, _):
+                m = 4 * j + i
+                far[core, m, 256:384] = (r2[m].astype(F32) * bit[2]).astype(BF)
+                return 0
+
+            lax.fori_loop(0, 4, body, 0)
+            start(es[j])
+
+        return event
+
+    def ev_es(j):
+        return es[j].wait_recv
 
     def ev_w2():
         for p in (0, 1):
@@ -315,8 +364,9 @@
             start(wsteps[p][6])
 
     def probs_body(h, _):
-        wr = rolled(h) * SCALE
-        ws = [wr[:, 16 * l : 16 * l + 1] for l in range(7)]
+        wr = rolled(h)
+        scaled = wr * SCALE
+        ws = [(scaled if l < 3 else wr)[:, 16 * l : 16 * l + 1] for l in range(7)]
         qh, kh = q_v[:, hcols(h)], k_v[:, hcols(h)]
         for blk in (0, 1):
             r0 = 256 * blk
@@ -335,45 +385,42 @@
         wq[h, 256:512, 384:512] = (qf[256:] * ws[3][256:]).astype(BF)
         return 0
 
-    def run(body, cuts):
-        at = 0
-        for stop, event in cuts:
-            if stop > at:
-                lax.fori_loop(at, stop, body, 0)
-            at = stop
-            if event is not None:
-                event()
-
-    run(probs_body, [(3, ev_e0), (5, ev_w2), (11, ev_e1), (13, ev_w3), (16, None)])
-    ev_e2()
-    e1s.wait_recv()
-    e2s.wait_recv()
+    run(
+        probs_body,
+        [
+            (1, ev_e0(0)), (2, ev_w2), (3, ev_e0(1)), (7, ev_e1(0)), (11, ev_e1(1)),
+            (14, ev_e2(0)), (15, ev_w3), (16, ev_es(0)),
+        ],
+    )
 
     def attn_copy(h):
         return pltpu.make_async_remote_copy(
-            src_ref=attn.at[0, h], dst_ref=attn.at[1, h], send_sem=asem.at[h],
+            src_ref=own_v.at[:, hcols(h)], dst_ref=attn_sib.at[h], send_sem=asem.at[h],
             recv_sem=arsem.at[h], device_id=sib, device_id_type=MESH,
         )
 
-    def attn_body(h, _):
+    def attn_body(i, _):
+        hi, lo = chunked(i)
+        h = hi * 8 + lo
         vh = v_v[:, hcols(h)]
-        cross = dot(wq[h], far[h], 1, 0)
+        cross = dot(wq[h], far[hi, lo], 1, 0) * SCALE
         for blk in (0, 1):
             r0 = 256 * blk
             out = dot(probs[h, blk], vh[r0 : r0 + 256], 1, 0) + cross[r0 : r0 + 256]
-            attn[0, h, r0 : r0 + 256] = out.astype(BF)
+            own_v[r0 : r0 + 256, hcols(h)] = out.astype(BF)
         attn_copy(h).start()
         return 0
 
-    lax.fori_loop(0, H, attn_body, 0)
+    run(attn_body, [(4, ev_e2(1)), (8, ev_es(1)), (16,)])
 
     loads[4].wait()
     dcopy.wait_recv()
 
-    def wg_body(h, _):
+    def wg_body(i, _):
+        h = head(i)
         attn_copy(h).wait_recv()
         own = d_v[:, pl.ds(pl.multiple_of(core * HALF, HALF), HALF)]
-        part = dot(attn[0, h], own, 0, 0) + dot(attn[1, h], dosib[...], 0, 0)
+        part = dot(own_v[:, hcols(h)], own, 0, 0) + dot(attn_sib[h], dosib[...], 0, 0)
         part = part.astype(BF)
         zd = rem(div(h, 4) + core, 4)
         cd = rem(div(h, 2), 2)
@@ -386,64 +433,77 @@
                     accs[piece][zd, xd, yd, cd] = part[row : row + 16, c0_ : c0_ + width]
         return 0
 
-    lax.fori_loop(0, H, wg_body, 0)
+    run(wg_body, [(10, ev_w4), (16,)])
     rs_start(0)
 
-    ev_w4()
     for p in (0, 1):
         for i in (4, 5, 6):
             wsteps[p][i].wait_recv()
 
     def g_body(i, _):
         blocks = []
+        hi, lo = chunked(2 * i)
         for j in (0, 1):
-            h = 2 * i + j
+            h = hi * 8 + lo + j
             hx, hy = div(h, 4), rem(h, 4)
             hx1, hy1 = rem(hx + 1, 4), rem(hy + 1, 4)
             blocks += [w_g[0, 0, hx, hy], w_g[0, 1, hx1, hy1], w_g[1, 0, hy, hx], w_g[1, 1, hy1, hx1]]
         weight = jnp.concatenate(blocks, axis=0)
         out = dot(d_v[...], weight, 1, 1).astype(BF)
         for j in (0, 1):
-            h = 2 * i + j
+            h = hi * 8 + lo + j
             gh = out[:, 128 * j : 128 * j + 128]
             g_v[h] = gh
             grads = dot(gh, wq[h], 0, 0)
             for b in range(3):
-                gt[b, h] = (grads[:, 128 * b : 128 * b + 128] * bit[b]).astype(BF)
-            gt[3, h] = grads[:, 384:512].astype(BF)
+                gt[b, hi, lo + j] = (grads[:, 128 * b : 128 * b + 128] * (bit[b] * SCALE)).astype(BF)
+            gt[3, hi, lo + j] = (grads[:, 384:512] * SCALE).astype(BF)
         return 0
 
-    lax.fori_loop(0, H // 2, g_body, 0)
-    start(c0)
-    start(c12)
-
-    def ev_c12():
-        c12.wait_recv()
-
-        def body(i, _):
-            for b in (0, 1):
-                cs12[b, i] = (gt[1 + b, core * 8 + i].astype(F32) + recv12[b, i].astype(F32)).astype(BF)
-            return 0
-
-        lax.fori_loop(0, 8, body, 0)
-        start(c1)
-        start(c2)
-
-    def ev_c2():
-        c2.wait_recv()
-        start(c3)
-
-    def ev_c3():
-        c1.wait_recv()
-        c3.wait_recv()
-
-        def body(i, _):
-            total = r1b[i].astype(F32) + r2b[i].astype(F32) + r3b[i].astype(F32)
-            sgsum[core * 8 + i] = total.astype(BF)
-            return 0
-
-        lax.fori_loop(0, 8, body, 0)
-        start(c4)
+    def ev_c12(j):
+        def event():
+            c12[j].wait_recv()
+
+            def body(i, _):
+                m = 4 * j + i
+                for b in (0, 1):
+                    both = gt[1 + b, core, m].astype(F32) + recv12[b, m].astype(F32)
+                    cs12[b, m] = both.astype(BF)
+                return 0
+
+            lax.fori_loop(0, 4, body, 0)
+            start(c1[j])
+            start(c2[j])
+
+        return event
+
+    def ev_c2(j):
+        def event():
+            c2[j].wait_recv()
+            start(c3[j])
+
+        return event
+
+    def ev_c3(j):
+        def event():
+            c1[j].wait_recv()
+            c3[j].wait_recv()
+
+            def body(i, _):
+                m = 4 * j + i
+                both = r1b[m].astype(F32) + r2b[m].astype(F32) + r3b[m].astype(F32)
+                sgsum[core, m] = both.astype(BF)
+                return 0
+
+            lax.fori_loop(0, 4, body, 0)
+            start(c4[j])
+
+        return event
+
+    run(
+        g_body,
+        [(4, starts(c0[0], c12[0])), (5, ev_c12(0)), (8, starts(c0[1], c12[1]))],
+    )
 
     def ev_rs(n):
         def event():
@@ -465,20 +525,21 @@
     dfar = lax.broadcasted_iota(jnp.int32, (512, 128), 1) - 64 - 16 * div(frow, 128)
 
     def dq_body(h, _):
-        wr = rolled(h) * SCALE
+        wr = rolled(h)
         ws = [wr[:, 16 * l : 16 * l + 1] for l in range(7)]
         qf = q_v[:, hcols(h)].astype(F32)
         kh, vh, gh = k_v[:, hcols(h)], v_v[:, hcols(h)], g_v[h]
+        fh = far.at[div(h, 8), rem(h, 8)]
         sel = (dsel == h).astype(F32).astype(BF)
         fsel = (dfar == h).astype(F32).astype(BF)
         dq = None
         prods = []
         for b in range(3):
-            pb = dot(gh, far[h, 128 * b : 128 * b + 128], 1, 1)
+            pb = dot(gh, fh[128 * b : 128 * b + 128], 1, 1)
             prods.append((qf * pb).astype(BF))
             term = pb * ws[4 + b]
             dq = term if dq is None else dq + term
-        p3 = dot(gh[256:], far[h, 384:512], 1, 1)
+        p3 = dot(gh[256:], fh[384:512], 1, 1)
         prod3 = (qf[256:] * p3).astype(BF)
         p3 = p3 * ws[3][256:]
         for blk in (0, 1):
@@ -506,34 +567,47 @@
                 sums = dot(jnp.concatenate(fars, axis=1), fsel, 1, 0)
             else:
                 sums = dot(jnp.concatenate(fars, axis=1), fsel[:384], 1, 0)
-            attn[0, h, r0 : r0 + 256] = out.astype(BF)
+            own_v[r0 : r0 + 256, hcols(h)] = (out * SCALE).astype(BF)
             tacc[r0 : r0 + 256] += sums + dot(energy, sel, 1, 0)
-        pltpu.make_async_copy(attn.at[0, h], dq_out.at[0, :, hcols(h)], lsem.at[8 + h]).start()
         return 0
 
     run(
         dq_body,
-        [(1, ev_c12), (6, ev_c2), (8, ev_rs(0)), (11, ev_rs(1)), (12, ev_c3), (14, ev_rs(2)), (15, ev_rs(3)), (16, None)],
+        [
+            (1, ev_rs(0), ev_c12(1)), (3, ev_c2(0)), (6, ev_rs(1)), (7, ev_c2(1)), (8, ev_c3(0)),
+            (10, ev_rs(2)), (12, ev_rs(3), ev_c3(1)), (14, ev_rs(4)), (16,),
+        ],
     )
-    c0.wait_recv()
-    c4.wait_recv()
+    for j in (0, 1):
+        c0[j].wait_recv()
+        c4[j].wait_recv()
 
     def dk_body(h, _):
-        base = sg0[h].astype(F32) + sgsum[h].astype(F32)
-        halves = ((base + gt[3, h].astype(F32)).astype(BF), base.astype(BF))
+        hi, lo = div(h, 8), rem(h, 8)
+        base = sg0[hi, lo].astype(F32) + sgsum[hi, lo].astype(F32)
+        halves = ((base + gt[3, hi, lo].astype(F32)).astype(BF), base.astype(BF))
         for blk in (0, 1):
             rows = pl.ds(256 * blk, 256)
             kb, vb, qb = k_v[rows, hcols(h)], v_v[rows, hcols(h)], q_v[rows, hcols(h)]
             gb = g_v[h, rows]
             dv = dot(probs[h, blk], gb, 0, 0) + dot(kb, halves[blk], 1, 1)
-            dk = dot(wq[h, rows, 0:256], qb, 0, 0) + dot(vb, halves[blk], 1, 0)
+            dk = dot(wq[h, rows, 0:256], qb, 0, 0) * SCALE + dot(vb, halves[blk], 1, 0)
             k_v[rows, hcols(h)] = dk.astype(BF)
             v_v[rows, hcols(h)] = dv.astype(BF)
-        pltpu.make_async_copy(k_v.at[:, hcols(h)], dk_out.at[0, :, hcols(h)], lsem.at[24 + h]).start()
-        pltpu.make_async_copy(v_v.at[:, hcols(h)], dv_out.at[0, :, hcols(h)], lsem.at[40 + h]).start()
         return 0
 
-    run(dk_body, [(6, ev_rs(4)), (16, None)])
+    def finish():
+        for piece, (first, width) in enumerate(COLS):
+            rs_copies[piece][5].wait_recv()
+            f32s, recv = kept[piece], recvs[piece][5]
+            at = tuple(s.start for s in rs_kept[piece][5])
+            cols = slice(first, first + width)
+            wgout[core, :, cols] = f32s[at + (core,)] + recv[0, 0, 0, core].astype(F32)
+            finsend[:, cols] = f32s[at + (1 - core,)] + recv[0, 0, 0, 1 - core].astype(F32)
+        start(last)
+
+    last = remote(50, finsend, wgout.at[core], sib)
+    run(dk_body, [(6, finish), (16,)])
 
     lane = lax.broadcasted_iota(jnp.int32, (64, 128), 1)
     for i in range(8):
@@ -555,80 +629,52 @@
             res = jnp.where((lane >= 48) & (lane < 64), moved(7, 3) * SCALE, res)
         res = jnp.where((lane >= 64) & (lane < 112), t * SCALE, res)
         tacc[rows] = res
-    gcopy = pltpu.make_async_copy(tacc, gain_out.at[0], lsem.at[56])
-    gcopy.start()
-
-    for piece, (c0_, width) in enumerate(COLS):
-        rs_copies[piece][5].wait_recv()
-        acc, recv = accs[piece], recvs[piece][5]
-        own_at = (rot[0], rot[1], rot[2], core)
-        sib_at = (rot[0], rot[1], rot[2], 1 - core)
-        wgout[core, :, c0_ : c0_ + width] = acc[own_at].astype(F32) + recv[0, 0, 0, core].astype(F32)
-        finsend[:, c0_ : c0_ + width] = acc[sib_at].astype(F32) + recv[0, 0, 0, 1 - core].astype(F32)
-    last = remote(50, finsend, wgout.at[core], sib)
-    start(last)
     last.wait_recv()
-    outs = [
-        pltpu.make_async_copy(wgout.at[i], wg_out.at[:, pl.ds(HALF * i, HALF)], lsem.at[57 + i])
-        for i in (0, 1)
-    ]
-    for c in outs:
-        c.start()
+    for i in (0, 1):
+        wg_out[:, HALF * i : HALF * i + HALF] = wgout[i]
     for c in sent:
         c.wait_send()
 
-    def wait_out(h, _):
-        pltpu.make_async_copy(attn.at[0, h], dq_out.at[0, :, hcols(h)], lsem.at[8 + h]).wait()
-        pltpu.make_async_copy(k_v.at[:, hcols(h)], dk_out.at[0, :, hcols(h)], lsem.at[24 + h]).wait()
-        pltpu.make_async_copy(v_v.at[:, hcols(h)], dv_out.at[0, :, hcols(h)], lsem.at[40 + h]).wait()
-        return 0
-
-    lax.fori_loop(0, H, wait_out, 0)
-    gcopy.wait()
-    for c in outs:
-        c.wait()
-
 
 def local(queries, keys, values, level_gain, out_weight, out_grad):
-    big = jax.ShapeDtypeStruct((1, T, D), BF)
+    big = pltpu.VMEM((1, T, D), BF)
+    state = (2, 8, HD, HD)
     scratch = [
-        pltpu.VMEM((T, D), BF),
-        pltpu.VMEM((T, D), BF),
         pltpu.VMEM((T, D), BF),
         pltpu.VMEM((T, D), BF),
         pltpu.VMEM((T, HD), F32),
         pltpu.VMEM((2, 2, 4, 4, 32, D), BF),
-        pltpu.VMEM((2, H, T, HD), BF),
+        pltpu.VMEM((H, T, HD), BF),
         pltpu.VMEM((T, HALF), BF),
         pltpu.VMEM((H, T, T), BF),
         pltpu.VMEM((H, 2, 256, 256), BF),
         pltpu.VMEM((H, T, HD), BF),
-        pltpu.VMEM((H, T, HD), BF),
-        pltpu.VMEM((H, HD, HD), F32),
-        pltpu.VMEM((H, HD, HD), BF),
-        pltpu.VMEM((H, HD, HD), BF),
+        pltpu.VMEM((2, 8, T, HD), BF),
+        pltpu.VMEM(state, F32),
+        pltpu.VMEM(state, F32),
+        pltpu.VMEM((8, HD, HD), F32),
         pltpu.VMEM((8, HD, HD), BF),
         pltpu.VMEM((8, HD, HD), BF),
         pltpu.VMEM((8, HD, HD), BF),
         pltpu.VMEM((8, HD, HD), BF),
-        pltpu.VMEM((4, H, HD, HD), BF),
-        pltpu.VMEM((H, HD, HD), BF),
-        pltpu.VMEM((2, 8, HD, HD), BF),
-        pltpu.VMEM((2, 8, HD, HD), BF),
+        pltpu.VMEM((4,) + state, BF),
+        pltpu.VMEM(state, BF),
+        pltpu.VMEM(state, BF),
+        pltpu.VMEM(state, BF),
         pltpu.VMEM((8, HD, HD), BF),
         pltpu.VMEM((8, HD, HD), BF),
         pltpu.VMEM((8, HD, HD), BF),
-        pltpu.VMEM((H, HD, HD), BF),
-        pltpu.VMEM((T, HD), F32),
+        pltpu.VMEM(state, BF),
         pltpu.VMEM((2, 16, HALF), F32),
         pltpu.VMEM((16, HALF), F32),
     ]
     scratch += [pltpu.VMEM((4, 4, 4, 2, 16, width), BF) for _, width in COLS]
+    scratch += [pltpu.VMEM(shape, F32) for shape in recv_shapes()[::6]]
     scratch += [pltpu.VMEM(shape, BF) for shape in recv_shapes()]
     scratch += [
-        pltpu.SemaphoreType.DMA((60,)),
-        pltpu.SemaphoreType.DMA((52,)),
-        pltpu.SemaphoreType.DMA((52,)),
+        pltpu.SemaphoreType.DMA((8,)),
+        pltpu.SemaphoreType.DMA((72,)),
+        pltpu.SemaphoreType.DMA((72,)),
         pltpu.SemaphoreType.DMA((H,)),
         pltpu.SemaphoreType.DMA((H,)),
     ]
@@ -637,14 +683,14 @@
         kernel,
         out_shape=(
             big, big, big,
-            jax.ShapeDtypeStruct((1, T, HD), F32),
-            jax.ShapeDtypeStruct((16, D), F32),
+            pltpu.VMEM((1, T, HD), F32),
+            pltpu.VMEM((16, D), F32),
         ),
         in_specs=[anyspace] * 6,
-        out_specs=(anyspace,) * 5,
+        out_specs=(pl.BlockSpec(memory_space=pltpu.VMEM),) * 5,
         scratch_shapes=scratch,
         compiler_params=pltpu.CompilerParams(
-            collective_id=0, has_side_effects=True, vmem_limit_bytes=62 * 2**20
+            collective_id=0, has_side_effects=True, vmem_limit_bytes=57 * 2**20
         ),
         cost_estimate=pl.CostEstimate(flops=20 * 10**9, bytes_accessed=16 * 2**20, transcendentals=0),
     )(queries, keys, values, level_gain, out_weight, out_grad)

time: 109 us -> 96.5 us (0.89)
  the two profiles are of different devices: /device:TPU:1 before, /device:TPU:2 now
where the time goes in v2:
time: 96.5 us; the launch traced here: 96.4 us
  Pallas kernels  90.4 us (94%)
  local copies, waits for them, and re-layouts  5.32 us (6%)
    pallas_call x1, Pallas kernels, local(): pl.pallas_call(kernel, out_shape=(big, big, big, pltpu.VMEM((1, T, HD), F...  90.4 us
    unnamed x5, local copies, waits for them, and re-layouts  5.32 us

profile of v2, /device:TPU:2, one launch (start us, length us, event | category | flops | bytes accessed | tf_op | source)
XLA Modules:
  0.0 96.4 jit_solution(6151995654584380757)
XLA Ops:
  0.6 90.4 %shard_map.101 = (bf16[1,512,2048]{2,1,0:T(8,128)(2,1)S(1)}, bf16[1,512,2048]{2,1,0:T(8,128)(2,1)S(1)}, bf16[1,512,2048]{2,1,0:T(8,128)(2,1)S(1)}, f32[1,512,128]{2,1,0:T(8,128)S(1)}, f32[16,2048]{1,0:T(8,128)S(1)}) custom-call(bf16[1,512,2048]{2,1,0:T(8,128)(2,1)} %q_in.1, bf16[1,512,2048]{2,1,0:T(8,128)(2,1)} %k_in.1, bf16[1,512,2048]{2,1,0:T(8,128)(2,1)} %v_in.1, ...), custom_call_target="tpu_custom_call" | custom-call | flops 20000000000 | bytes 16777216 | tf_op jit(solution)/shard_map/pallas_call | solution.py:682
  91.0 1.3 %copy.16 = bf16[1,512,2048]{2,1,0:T(8,128)(2,1)} copy(bf16[1,512,2048]{2,1,0:T(8,128)(2,1)S(1)} %get-tuple-element.5) | data formatting | bytes 4194304
  92.4 0.7 copy.20
  93.0 0.7 copy.19
  93.7 1.3 %copy.17 = bf16[1,512,2048]{2,1,0:T(8,128)(2,1)} copy(bf16[1,512,2048]{2,1,0:T(8,128)(2,1)S(1)} %get-tuple-element.6) | data formatting | bytes 4194304
  95.0 1.3 %copy.18 = bf16[1,512,2048]{2,1,0:T(8,128)(2,1)} copy(bf16[1,512,2048]{2,1,0:T(8,128)(2,1)S(1)} %get-tuple-element.7) | data formatting | bytes 4194304

commit v3 on v2

--- a/solution.py
+++ b/solution.py
@@ -49,7 +49,7 @@
     q_in, k_in, v_in, gain_in, w_in, d_in,
     dq_out, dk_out, dv_out, gain_out, wg_out,
     q_v, d_v, gain_v, w_g, attn_sib, dosib, wq, probs, g_v, far,
-    st, st_sib, total, cs_send, r1, run_send, r2,
+    st, st_sib, cs_send, r1, r2, r3,
     gt, sg0, recv12, cs12, r1b, r2b, r3b, sgsum, wgout, finsend,
     acc0, acc1, acc2, fk0, fk1, fk2,
     *rest,
@@ -88,35 +88,36 @@
             o1, o2 = rem(c1 + 4 - p, 4), rem(c2 + 4 - p, 4)
             return (seq, (o1 * 4 + o2) * (1 - core) + (o2 * 4 + o1) * core)
 
-        own = w_in.at[pl.ds(pl.multiple_of(core * 64 + p * 32, 32), 32), :]
-        wloads.append(load(5 + p, own, w_g.at[core, p, b1, b2]))
+        own32 = w_in.at[pl.ds(pl.multiple_of(core * 64 + p * 32, 32), 32), :]
+        wloads.append(load(5 + p, own32, w_g.at[core, p, b1, b2]))
         pair1, pair2 = div(b1, 2) * 2, div(b2, 2) * 2
-        base = 10 * p
-        steps = []
-
-        def add(src, dst, device, base=base, steps=steps):
-            i = base + len(steps)
-            steps.append(
-                pltpu.make_async_remote_copy(
-                    src_ref=src, dst_ref=dst, send_sem=ssem.at[i], recv_sem=rsem.at[i],
-                    device_id=device, device_id_type=MESH,
+        for k in (0, 1):
+            sub = pl.ds(16 * k, 16)
+            own = w_in.at[pl.ds(pl.multiple_of(core * 64 + p * 32 + k * 16, 16), 16), :]
+            steps = []
+
+            def add(src, dst, device, base=80 + (p * 2 + k) * 7, steps=steps):
+                i = base + len(steps)
+                steps.append(
+                    pltpu.make_async_remote_copy(
+                        src_ref=src, dst_ref=dst, send_sem=ssem.at[i], recv_sem=rsem.at[i],
+                        device_id=device, device_id_type=MESH,
+                    )
                 )
-            )
-
-        one = w_g.at[core, p, b1, b2]
-        add(own, one, dev(flip(b1), b2))
-        two = w_g.at[core, p, pl.ds(pair1, 2), b2]
-        add(two, two, dev(3 - b1, b2))
-        four = w_g.at[core, p, :, b2]
-        add(four, four, dev(b1, flip(b2)))
-        eight = w_g.at[core, p, :, pl.ds(pair2, 2)]
-        add(eight, eight, dev(b1, 3 - b2))
-        add(four, four, sib)
-        four2 = w_g.at[core, p, :, flip(b2)]
-        add(four2, four2, sib)
-        eight2 = w_g.at[core, p, :, pl.ds(2 - pair2, 2)]
-        add(eight2, eight2, sib)
-        wsteps.append(steps)
+
+            add(own, w_g.at[core, p, b1, b2, sub], dev(flip(b1), b2))
+            two = w_g.at[core, p, pl.ds(pair1, 2), b2, sub]
+            add(two, two, dev(3 - b1, b2))
+            four = w_g.at[core, p, :, b2, sub]
+            add(four, four, dev(b1, flip(b2)))
+            eight = w_g.at[core, p, :, pl.ds(pair2, 2), sub]
+            add(eight, eight, dev(b1, 3 - b2))
+            add(four, four, sib)
+            four2 = w_g.at[core, p, :, flip(b2), sub]
+            add(four2, four2, sib)
+            eight2 = w_g.at[core, p, :, pl.ds(2 - pair2, 2), sub]
+            add(eight2, eight2, sib)
+            wsteps.append(steps)
     for c in wloads:
         c.start()
 
@@ -125,7 +126,7 @@
         sib,
         (seq, flip(x) * 4 + y), (seq, (3 - x) * 4 + y),
         (seq, x * 4 + flip(y)), (seq, x * 4 + 3 - y),
-        (flip(z) * 2 + core, bat), ((3 - z) * 2 + core, bat),
+        (flip(z) * 2 + core, bat), ((3 - z) * 2 + core, bat), (rem(z + 2, 4) * 2 + core, bat),
     ]
     for n in neighbours:
         pl.semaphore_signal(barrier, inc=1, device_id=n, device_id_type=MESH)
@@ -143,8 +144,9 @@
         c.start()
         sent.append(c)
 
-    for p in (0, 1):
-        start(wsteps[p][0])
+    for k in (0, 1):
+        for p in (0, 1):
+            start(wsteps[2 * p + k][0])
 
     dcopy = remote(
         20, d_in.at[0, :, pl.ds(pl.multiple_of((1 - core) * HALF, HALF), HALF)], dosib, sib
@@ -153,20 +155,22 @@
 
     zp1 = (flip(z) * 2 + core, bat)
     zp3 = ((3 - z) * 2 + core, bat)
-    e0, e1, e2, es, c0, c12, c1, c2, c3, c4 = [[] for _ in range(10)]
+    zp2 = (rem(z + 2, 4) * 2 + core, bat)
+    e0, e1, e2, e3, es, c0, c12, c1, c2, c3, c4 = [[] for _ in range(11)]
     for j in (0, 1):
         four = pl.ds(4 * j, 4)
-        n = 51 + 10 * j
+        n = 51 + 11 * j
         e0.append(remote(n, st.at[:, four], st_sib.at[:, four], sib))
         e1.append(remote(n + 1, cs_send.at[four], r1.at[four], zp1))
-        e2.append(remote(n + 2, run_send.at[four], r2.at[four], zp3))
+        e2.append(remote(n + 2, cs_send.at[four], r2.at[four], zp3))
+        e3.append(remote(n + 10, cs_send.at[four], r3.at[four], zp2))
         fars = far.at[core, four, pl.ds(128, 256)]
         es.append(remote(n + 3, fars, fars, sib))
         c0.append(remote(n + 4, gt.at[0, :, four], sg0.at[:, four], sib))
         c12.append(remote(n + 5, gt.at[pl.ds(1, 2), 1 - core, four], recv12.at[:, four], sib))
         c1.append(remote(n + 6, cs12.at[0, four], r1b.at[four], zp1))
         c2.append(remote(n + 7, cs12.at[1, four], r2b.at[four], zp3))
-        c3.append(remote(n + 8, r2b.at[four], r3b.at[four], zp1))
+        c3.append(remote(n + 8, cs12.at[1, four], r3b.at[four], zp2))
         sums = sgsum.at[core, four]
         c4.append(remote(n + 9, sums, sums, sib))
     bit = [rem(seq, 2).astype(F32), rem(z, 2).astype(F32), div(z, 2).astype(F32)]
@@ -260,20 +264,39 @@
         st[hi, lo] = low + dot(kh[256:], vh[256:], 0, 0)
         return 0
 
-    def ev_w1():
-        for p in (0, 1):
-            wloads[p].wait()
-            wsteps[p][0].wait_recv()
-            start(wsteps[p][1])
-
-    def run(body, cuts):
-        at = 0
-        for stop, *events in cuts:
-            if stop > at:
-                lax.fori_loop(at, stop, body, 0)
-            at = stop
-            for event in events:
-                event()
+    def ev_w(n, k):
+        def event():
+            for p in (0, 1):
+                steps = wsteps[2 * p + k]
+                if n == 1 and k == 0:
+                    wloads[p].wait()
+                steps[n - 1].wait_recv()
+                if n < 4:
+                    start(steps[n])
+                if n > 1:
+                    start(steps[n + 2])
+
+        return event
+
+    def run(body, cuts, count=H, step=1):
+        def stepped(i, _):
+            for at, *events in cuts:
+                if at < count:
+
+                    @pl.when(i * step == at)
+                    def _():
+                        for event in events:
+                            event()
+
+            for j in range(step):
+                body(i * step + j, 0)
+            return 0
+
+        lax.fori_loop(0, count // step, stepped, 0)
+        for at, *events in cuts:
+            if at >= count:
+                for event in events:
+                    event()
 
     def starts(*copies):
         def event():
@@ -282,7 +305,11 @@
 
         return event
 
-    run(state_body, [(4, ev_w1), (8, starts(e0[0])), (16, starts(e0[1]))])
+    run(
+        state_body,
+        [(4, ev_w(1, 0)), (8, starts(e0[0]), ev_w(1, 1)), (16, starts(e0[1]))],
+        step=2,
+    )
     loads[2].wait()
     loads[3].wait()
 
@@ -303,39 +330,26 @@
                 m = 4 * j + i
                 for hi in (0, 1):
                     far[hi, m, 0:128] = (st_sib[hi, m] * bit[0]).astype(BF)
-                chip = st[core, m] + st_sib[core, m]
-                total[m] = chip
-                cs_send[m] = chip.astype(BF)
+                cs_send[m] = (st[core, m] + st_sib[core, m]).astype(BF)
                 return 0
 
             lax.fori_loop(0, 4, body, 0)
             start(e1[j])
+            start(e2[j])
+            start(e3[j])
 
         return event
 
     def ev_e1(j):
         def event():
             e1[j].wait_recv()
+            e2[j].wait_recv()
+            e3[j].wait_recv()
 
             def body(i, _):
                 m = 4 * j + i
-                got = r1[m].astype(F32)
-                far[core, m, 128:256] = (got * bit[1]).astype(BF)
-                run_send[m] = (total[m] + got).astype(BF)
-                return 0
-
-            lax.fori_loop(0, 4, body, 0)
-            start(e2[j])
-
-        return event
-
-    def ev_e2(j):
-        def event():
-            e2[j].wait_recv()
-
-            def body(i, _):
-                m = 4 * j + i
-                far[core, m, 256:384] = (r2[m].astype(F32) * bit[2]).astype(BF)
+                far[core, m, 128:256] = (r1[m].astype(F32) * bit[1]).astype(BF)
+                far[core, m, 256:384] = ((r2[m].astype(F32) + r3[m].astype(F32)) * bit[2]).astype(BF)
                 return 0
 
             lax.fori_loop(0, 4, body, 0)
@@ -345,23 +359,6 @@
 
     def ev_es(j):
         return es[j].wait_recv
-
-    def ev_w2():
-        for p in (0, 1):
-            wsteps[p][1].wait_recv()
-            start(wsteps[p][2])
-            start(wsteps[p][4])
-
-    def ev_w3():
-        for p in (0, 1):
-            wsteps[p][2].wait_recv()
-            start(wsteps[p][3])
-            start(wsteps[p][5])
-
-    def ev_w4():
-        for p in (0, 1):
-            wsteps[p][3].wait_recv()
-            start(wsteps[p][6])
 
     def probs_body(h, _):
         wr = rolled(h)
@@ -388,8 +385,8 @@
     run(
         probs_body,
         [
-            (1, ev_e0(0)), (2, ev_w2), (3, ev_e0(1)), (7, ev_e1(0)), (11, ev_e1(1)),
-            (14, ev_e2(0)), (15, ev_w3), (16, ev_es(0)),
+            (1, ev_e0(0)), (2, ev_w(2, 0)), (4, ev_e0(1), ev_w(2, 1)), (11, ev_w(3, 0)),
+            (14, ev_e1(0)), (16, ev_w(3, 1), ev_es(0)),
         ],
     )
 
@@ -411,7 +408,7 @@
         attn_copy(h).start()
         return 0
 
-    run(attn_body, [(4, ev_e2(1)), (8, ev_es(1)), (16,)])
+    run(attn_body, [(4, ev_e1(1)), (8, ev_es(1)), (16, ev_w(4, 0))], step=2)
 
     loads[4].wait()
     dcopy.wait_recv()
@@ -433,12 +430,12 @@
                     accs[piece][zd, xd, yd, cd] = part[row : row + 16, c0_ : c0_ + width]
         return 0
 
-    run(wg_body, [(10, ev_w4), (16,)])
+    run(wg_body, [(13, ev_w(4, 1))])
     rs_start(0)
 
-    for p in (0, 1):
+    for steps in wsteps:
         for i in (4, 5, 6):
-            wsteps[p][i].wait_recv()
+            steps[i].wait_recv()
 
     def g_body(i, _):
         blocks = []
@@ -474,12 +471,6 @@
             lax.fori_loop(0, 4, body, 0)
             start(c1[j])
             start(c2[j])
-
-        return event
-
-    def ev_c2(j):
-        def event():
-            c2[j].wait_recv()
             start(c3[j])
 
         return event
@@ -487,6 +478,7 @@
     def ev_c3(j):
         def event():
             c1[j].wait_recv()
+            c2[j].wait_recv()
             c3[j].wait_recv()
 
             def body(i, _):
@@ -502,7 +494,8 @@
 
     run(
         g_body,
-        [(4, starts(c0[0], c12[0])), (5, ev_c12(0)), (8, starts(c0[1], c12[1]))],
+        [(4, starts(c0[0], c12[0])), (6, ev_c12(0)), (8, starts(c0[1], c12[1]))],
+        count=H // 2,
     )
 
     def ev_rs(n):
@@ -574,8 +567,8 @@
     run(
         dq_body,
         [
-            (1, ev_rs(0), ev_c12(1)), (3, ev_c2(0)), (6, ev_rs(1)), (7, ev_c2(1)), (8, ev_c3(0)),
-            (10, ev_rs(2)), (12, ev_rs(3), ev_c3(1)), (14, ev_rs(4)), (16,),
+            (2, ev_rs(0)), (3, ev_c12(1)), (6, ev_c3(0)), (9, ev_rs(1)), (13, ev_c3(1)),
+            (14, ev_rs(2)),
         ],
     )
     for j in (0, 1):
@@ -607,7 +600,7 @@
         start(last)
 
     last = remote(50, finsend, wgout.at[core], sib)
-    run(dk_body, [(6, finish), (16,)])
+    run(dk_body, [(4, ev_rs(3)), (10, ev_rs(4)), (16, finish)], step=2)
 
     lane = lax.broadcasted_iota(jnp.int32, (64, 128), 1)
     for i in range(8):
@@ -652,7 +645,6 @@
         pltpu.VMEM((2, 8, T, HD), BF),
         pltpu.VMEM(state, F32),
         pltpu.VMEM(state, F32),
-        pltpu.VMEM((8, HD, HD), F32),
         pltpu.VMEM((8, HD, HD), BF),
         pltpu.VMEM((8, HD, HD), BF),
         pltpu.VMEM((8, HD, HD), BF),
@@ -673,8 +665,8 @@
     scratch += [pltpu.VMEM(shape, BF) for shape in recv_shapes()]
     scratch += [
         pltpu.SemaphoreType.DMA((8,)),
-        pltpu.SemaphoreType.DMA((72,)),
-        pltpu.SemaphoreType.DMA((72,)),
+        pltpu.SemaphoreType.DMA((112,)),
+        pltpu.SemaphoreType.DMA((112,)),
         pltpu.SemaphoreType.DMA((H,)),
         pltpu.SemaphoreType.DMA((H,)),
     ]

time: 96.5 us -> 90.2 us (0.935)
  the two profiles are of different devices: /device:TPU:2 before, /device:TPU:1 now
where the time goes in v3:
time: 90.2 us; the launch traced here: 90.1 us
  Pallas kernels  84.1 us (93%)
  local copies, waits for them, and re-layouts  5.32 us (6%)
    pallas_call x1, Pallas kernels, local(): pl.pallas_call(kernel, out_shape=(big, big, big, pltpu.VMEM((1, T, HD), F...  84.1 us
    unnamed x5, local copies, waits for them, and re-layouts  5.32 us

profile of v3, /device:TPU:1, one launch (start us, length us, event | category | flops | bytes accessed | tf_op | source)
XLA Modules:
  0.0 90.1 jit_solution(7084944053652295129)
XLA Ops:
  0.6 84.1 %shard_map.101 = (bf16[1,512,2048]{2,1,0:T(8,128)(2,1)S(1)}, bf16[1,512,2048]{2,1,0:T(8,128)(2,1)S(1)}, bf16[1,512,2048]{2,1,0:T(8,128)(2,1)S(1)}, f32[1,512,128]{2,1,0:T(8,128)S(1)}, f32[16,2048]{1,0:T(8,128)S(1)}) custom-call(bf16[1,512,2048]{2,1,0:T(8,128)(2,1)} %q_in.1, bf16[1,512,2048]{2,1,0:T(8,128)(2,1)} %k_in.1, bf16[1,512,2048]{2,1,0:T(8,128)(2,1)} %v_in.1, ...), custom_call_target="tpu_custom_call" | custom-call | flops 20000000000 | bytes 16777216 | tf_op jit(solution)/shard_map/pallas_call | solution.py:674
  84.8 1.3 %copy.16 = bf16[1,512,2048]{2,1,0:T(8,128)(2,1)} copy(bf16[1,512,2048]{2,1,0:T(8,128)(2,1)S(1)} %get-tuple-element.5) | data formatting | bytes 4194304
  86.1 0.7 copy.20
  86.8 0.7 copy.19
  87.5 1.3 %copy.17 = bf16[1,512,2048]{2,1,0:T(8,128)(2,1)} copy(bf16[1,512,2048]{2,1,0:T(8,128)(2,1)S(1)} %get-tuple-element.6) | data formatting | bytes 4194304
  88.8 1.3 %copy.18 = bf16[1,512,2048]{2,1,0:T(8,128)(2,1)} copy(bf16[1,512,2048]{2,1,0:T(8,128)(2,1)S(1)} %get-tuple-element.7) | data formatting | bytes 4194304

commit v4 on v3

--- a/solution.py
+++ b/solution.py
@@ -75,8 +75,6 @@
         load(3, gain_in.at[0], gain_v),
         load(4, d_in.at[0], d_v),
     ]
-    for c in loads:
-        c.start()
 
     a1 = x * (1 - core) + y * core
     a2 = y * (1 - core) + x * core
@@ -118,7 +116,7 @@
             eight2 = w_g.at[core, p, :, pl.ds(2 - pair2, 2), sub]
             add(eight2, eight2, sib)
             wsteps.append(steps)
-    for c in wloads:
+    for c in wloads + loads[:2]:
         c.start()
 
     barrier = pltpu.get_barrier_semaphore()
@@ -151,7 +149,6 @@
     dcopy = remote(
         20, d_in.at[0, :, pl.ds(pl.multiple_of((1 - core) * HALF, HALF), HALF)], dosib, sib
     )
-    start(dcopy)
 
     zp1 = (flip(z) * 2 + core, bat)
     zp3 = ((3 - z) * 2 + core, bat)
@@ -246,6 +243,9 @@
 
     loads[0].wait()
     loads[1].wait()
+    for c in loads[2:]:
+        c.start()
+    start(dcopy)
 
     def chunked(i):
         j, r = div(i, 8), rem(i, 8)
@@ -365,16 +365,14 @@
         scaled = wr * SCALE
         ws = [(scaled if l < 3 else wr)[:, 16 * l : 16 * l + 1] for l in range(7)]
         qh, kh = q_v[:, hcols(h)], k_v[:, hcols(h)]
-        for blk in (0, 1):
-            r0 = 256 * blk
-            sc = dot(qh[r0 : r0 + 256], kh[r0 : r0 + 256], 1, 1)
-            a, b = slice(r0, r0 + 128), slice(r0 + 128, r0 + 256)
-            probs[h, blk, 0:128, 0:128] = (sc[:128, :128] * diag_mask(ws[0][a], ws[1][a])).astype(BF)
-            probs[h, blk, 0:128, 128:256] = jnp.zeros((128, 128), BF)
-            probs[h, blk, 128:256, 0:128] = (sc[128:, :128] * ws[2][b]).astype(BF)
-            probs[h, blk, 128:256, 128:256] = (
-                sc[128:, 128:] * diag_mask(ws[0][b], ws[1][b])
-            ).astype(BF)
+        for t in range(4):
+            blk, r0, c0_ = t // 2, 128 * t, 256 * (t // 2)
+            rows, inner = slice(r0, r0 + 128), slice(r0 - c0_, r0 - c0_ + 128)
+            sc = dot(qh[rows], kh[c0_ : r0 + 128], 1, 1)
+            diag = sc[:, -128:] * diag_mask(ws[0][rows], ws[1][rows])
+            probs[h, blk, inner, inner] = diag.astype(BF)
+            if t % 2 == 1:
+                probs[h, blk, inner, 0:128] = (sc[:, :128] * ws[2][rows]).astype(BF)
         qf = qh.astype(F32)
         for b in range(3):
             wq[h, :, 128 * b : 128 * b + 128] = (qf * ws[4 + b]).astype(BF)
@@ -401,10 +399,11 @@
         h = hi * 8 + lo
         vh = v_v[:, hcols(h)]
         cross = dot(wq[h], far[hi, lo], 1, 0) * SCALE
-        for blk in (0, 1):
-            r0 = 256 * blk
-            out = dot(probs[h, blk], vh[r0 : r0 + 256], 1, 0) + cross[r0 : r0 + 256]
-            own_v[r0 : r0 + 256, hcols(h)] = out.astype(BF)
+        for t in range(4):
+            blk, r0, c0_ = t // 2, 128 * t, 256 * (t // 2)
+            near = probs[h, blk, r0 - c0_ : r0 - c0_ + 128, 0 : r0 - c0_ + 128]
+            out = dot(near, vh[c0_ : r0 + 128], 1, 0) + cross[r0 : r0 + 128]
+            own_v[r0 : r0 + 128, hcols(h)] = out.astype(BF)
         attn_copy(h).start()
         return 0
 
@@ -492,18 +491,18 @@
 
         return event
 
-    run(
-        g_body,
-        [(4, starts(c0[0], c12[0])), (6, ev_c12(0)), (8, starts(c0[1], c12[1]))],
-        count=H // 2,
-    )
-
     def ev_rs(n):
         def event():
             rs_add(n)
             rs_start(n + 1)
 
         return event
+
+    run(
+        g_body,
+        [(4, starts(c0[0], c12[0])), (6, ev_c12(0)), (8, starts(c0[1], c12[1]), ev_rs(0))],
+        count=H // 2,
+    )
 
     def wait_attn(h, _):
         attn_copy(h).wait_send()
@@ -535,40 +534,38 @@
         p3 = dot(gh[256:], fh[384:512], 1, 1)
         prod3 = (qf[256:] * p3).astype(BF)
         p3 = p3 * ws[3][256:]
+        far_sums = []
         for blk in (0, 1):
             r0 = 256 * blk
-            pg = dot(gh[r0 : r0 + 256], vh[r0 : r0 + 256], 1, 1)
-            a, b = slice(r0, r0 + 128), slice(r0 + 128, r0 + 256)
-            top = jnp.concatenate(
-                [(pg[:128, :128] * diag_mask(ws[0][a], ws[1][a])).astype(BF), jnp.zeros((128, 128), BF)], axis=1
-            )
-            bottom = jnp.concatenate(
-                [
-                    (pg[128:, :128] * ws[2][b]).astype(BF),
-                    (pg[128:, 128:] * diag_mask(ws[0][b], ws[1][b])).astype(BF),
-                ],
-                axis=1,
-            )
-            sg = jnp.concatenate([top, bottom], axis=0)
-            wq[h, r0 : r0 + 256, 0:256] = sg
-            energy = (pg * probs[h, blk].astype(F32)).astype(BF)
-            out = dot(sg, kh[r0 : r0 + 256], 1, 0) + dq[r0 : r0 + 256]
             fars = [prods[b][r0 : r0 + 256] for b in range(3)]
             if blk == 1:
-                out = out + p3
                 fars.append(prod3)
                 sums = dot(jnp.concatenate(fars, axis=1), fsel, 1, 0)
             else:
                 sums = dot(jnp.concatenate(fars, axis=1), fsel[:384], 1, 0)
-            own_v[r0 : r0 + 256, hcols(h)] = (out * SCALE).astype(BF)
-            tacc[r0 : r0 + 256] += sums + dot(energy, sel, 1, 0)
+            far_sums.append(sums)
+        for t in range(4):
+            blk, r0, c0_ = t // 2, 128 * t, 256 * (t // 2)
+            rows, inner = slice(r0, r0 + 128), slice(r0 - c0_, r0 - c0_ + 128)
+            width = r0 - c0_ + 128
+            pg = dot(gh[rows], vh[c0_ : r0 + 128], 1, 1)
+            sg = (pg[:, -128:] * diag_mask(ws[0][rows], ws[1][rows])).astype(BF)
+            if t % 2 == 1:
+                sg = jnp.concatenate([(pg[:, :128] * ws[2][rows]).astype(BF), sg], axis=1)
+            wq[h, rows, 0:width] = sg
+            energy = (pg * probs[h, blk, inner, 0:width].astype(F32)).astype(BF)
+            out = dot(sg, kh[c0_ : r0 + 128], 1, 0) + dq[rows]
+            if blk == 1:
+                out = out + p3[inner]
+            own_v[rows, hcols(h)] = (out * SCALE).astype(BF)
+            tacc[rows] += far_sums[blk][inner] + dot(energy, sel[:width], 1, 0)
         return 0
 
     run(
         dq_body,
         [
-            (2, ev_rs(0)), (3, ev_c12(1)), (6, ev_c3(0)), (9, ev_rs(1)), (13, ev_c3(1)),
-            (14, ev_rs(2)),
+            (2, ev_c12(1)), (5, ev_c3(0)), (7, ev_rs(1)), (12, ev_rs(2)), (13, ev_c3(1)),
+            (16, ev_rs(3)),
         ],
     )
     for j in (0, 1):
@@ -580,13 +577,14 @@
         base = sg0[hi, lo].astype(F32) + sgsum[hi, lo].astype(F32)
         halves = ((base + gt[3, hi, lo].astype(F32)).astype(BF), base.astype(BF))
         for blk in (0, 1):
-            rows = pl.ds(256 * blk, 256)
-            kb, vb, qb = k_v[rows, hcols(h)], v_v[rows, hcols(h)], q_v[rows, hcols(h)]
-            gb = g_v[h, rows]
-            dv = dot(probs[h, blk], gb, 0, 0) + dot(kb, halves[blk], 1, 1)
-            dk = dot(wq[h, rows, 0:256], qb, 0, 0) * SCALE + dot(vb, halves[blk], 1, 0)
-            k_v[rows, hcols(h)] = dk.astype(BF)
-            v_v[rows, hcols(h)] = dv.astype(BF)
+            for r0 in (256 * blk, 256 * blk + 128):
+                rows, after = slice(r0, r0 + 128), slice(r0, 256 * blk + 256)
+                inner = slice(r0 - 256 * blk, r0 - 256 * blk + 128)
+                kb, vb = k_v[rows, hcols(h)], v_v[rows, hcols(h)]
+                dv = dot(probs[h, blk, inner.start : 256, inner], g_v[h, after], 0, 0)
+                dk = dot(wq[h, after, inner], q_v[after, hcols(h)], 0, 0)
+                k_v[rows, hcols(h)] = (dk * SCALE + dot(vb, halves[blk], 1, 0)).astype(BF)
+                v_v[rows, hcols(h)] = (dv + dot(kb, halves[blk], 1, 1)).astype(BF)
         return 0
 
     def finish():
@@ -600,7 +598,7 @@
         start(last)
 
     last = remote(50, finsend, wgout.at[core], sib)
-    run(dk_body, [(4, ev_rs(3)), (10, ev_rs(4)), (16, finish)], step=2)
+    run(dk_body, [(6, ev_rs(4)), (14, finish)], step=2)
 
     lane = lax.broadcasted_iota(jnp.int32, (64, 128), 1)
     for i in range(8):

time: 90.2 us -> 91.5 us (1.014)
  Pallas kernels: 84.1 us -> 85.4 us
    pallas_call x1, Pallas kernels: 84.1 us -> 85.4 us  [local(): pl.pallas_call(kernel, out_shape=(big, big, big, pltpu.VMEM((1, T, HD), F...]
where the time goes in v4:
time: 91.5 us; the launch traced here: 91.4 us
  Pallas kernels  85.4 us (93%)
  local copies, waits for them, and re-layouts  5.32 us (6%)
    pallas_call x1, Pallas kernels, local(): pl.pallas_call(kernel, out_shape=(big, big, big, pltpu.VMEM((1, T, HD), F...  85.4 us
    unnamed x5, local copies, waits for them, and re-layouts  5.32 us

profile of v4, /device:TPU:1, one launch (start us, length us, event | category | flops | bytes accessed | tf_op | source)
XLA Modules:
  0.0 91.4 jit_solution(98349817855494962)
XLA Ops:
  0.6 85.4 %shard_map.101 = (bf16[1,512,2048]{2,1,0:T(8,128)(2,1)S(1)}, bf16[1,512,2048]{2,1,0:T(8,128)(2,1)S(1)}, bf16[1,512,2048]{2,1,0:T(8,128)(2,1)S(1)}, f32[1,512,128]{2,1,0:T(8,128)S(1)}, f32[16,2048]{1,0:T(8,128)S(1)}) custom-call(bf16[1,512,2048]{2,1,0:T(8,128)(2,1)} %q_in.1, bf16[1,512,2048]{2,1,0:T(8,128)(2,1)} %k_in.1, bf16[1,512,2048]{2,1,0:T(8,128)(2,1)} %v_in.1, ...), custom_call_target="tpu_custom_call" | custom-call | flops 20000000000 | bytes 16777216 | tf_op jit(solution)/shard_map/pallas_call | solution.py:672
  86.1 1.3 %copy.16 = bf16[1,512,2048]{2,1,0:T(8,128)(2,1)} copy(bf16[1,512,2048]{2,1,0:T(8,128)(2,1)S(1)} %get-tuple-element.5) | data formatting | bytes 4194304
  87.4 0.7 copy.20
  88.0 0.7 copy.19
  88.7 1.3 %copy.17 = bf16[1,512,2048]{2,1,0:T(8,128)(2,1)} copy(bf16[1,512,2048]{2,1,0:T(8,128)(2,1)S(1)} %get-tuple-element.6) | data formatting | bytes 4194304
  90.1 1.3 %copy.18 = bf16[1,512,2048]{2,1,0:T(8,128)(2,1)} copy(bf16[1,512,2048]{2,1,0:T(8,128)(2,1)S(1)} %get-tuple-element.7) | data formatting | bytes 4194304

commit v5 on v4

--- a/solution.py
+++ b/solution.py
@@ -75,6 +75,8 @@
         load(3, gain_in.at[0], gain_v),
         load(4, d_in.at[0], d_v),
     ]
+    for c in loads:
+        c.start()
 
     a1 = x * (1 - core) + y * core
     a2 = y * (1 - core) + x * core
@@ -116,7 +118,7 @@
             eight2 = w_g.at[core, p, :, pl.ds(2 - pair2, 2), sub]
             add(eight2, eight2, sib)
             wsteps.append(steps)
-    for c in wloads + loads[:2]:
+    for c in wloads:
         c.start()
 
     barrier = pltpu.get_barrier_semaphore()
@@ -149,6 +151,7 @@
     dcopy = remote(
         20, d_in.at[0, :, pl.ds(pl.multiple_of((1 - core) * HALF, HALF), HALF)], dosib, sib
     )
+    start(dcopy)
 
     zp1 = (flip(z) * 2 + core, bat)
     zp3 = ((3 - z) * 2 + core, bat)
@@ -243,9 +246,6 @@
 
     loads[0].wait()
     loads[1].wait()
-    for c in loads[2:]:
-        c.start()
-    start(dcopy)
 
     def chunked(i):
         j, r = div(i, 8), rem(i, 8)
@@ -365,14 +365,16 @@
         scaled = wr * SCALE
         ws = [(scaled if l < 3 else wr)[:, 16 * l : 16 * l + 1] for l in range(7)]
         qh, kh = q_v[:, hcols(h)], k_v[:, hcols(h)]
-        for t in range(4):
-            blk, r0, c0_ = t // 2, 128 * t, 256 * (t // 2)
-            rows, inner = slice(r0, r0 + 128), slice(r0 - c0_, r0 - c0_ + 128)
-            sc = dot(qh[rows], kh[c0_ : r0 + 128], 1, 1)
-            diag = sc[:, -128:] * diag_mask(ws[0][rows], ws[1][rows])
-            probs[h, blk, inner, inner] = diag.astype(BF)
-            if t % 2 == 1:
-                probs[h, blk, inner, 0:128] = (sc[:, :128] * ws[2][rows]).astype(BF)
+        for blk in (0, 1):
+            r0 = 256 * blk
+            sc = dot(qh[r0 : r0 + 256], kh[r0 : r0 + 256], 1, 1)
+            a, b = slice(r0, r0 + 128), slice(r0 + 128, r0 + 256)
+            probs[h, blk, 0:128, 0:128] = (sc[:128, :128] * diag_mask(ws[0][a], ws[1][a])).astype(BF)
+            probs[h, blk, 0:128, 128:256] = jnp.zeros((128, 128), BF)
+            probs[h, blk, 128:256, 0:128] = (sc[128:, :128] * ws[2][b]).astype(BF)
+            probs[h, blk, 128:256, 128:256] = (
+                sc[128:, 128:] * diag_mask(ws[0][b], ws[1][b])
+            ).astype(BF)
         qf = qh.astype(F32)
         for b in range(3):
             wq[h, :, 128 * b : 128 * b + 128] = (qf * ws[4 + b]).astype(BF)
@@ -399,11 +401,10 @@
         h = hi * 8 + lo
         vh = v_v[:, hcols(h)]
         cross = dot(wq[h], far[hi, lo], 1, 0) * SCALE
-        for t in range(4):
-            blk, r0, c0_ = t // 2, 128 * t, 256 * (t // 2)
-            near = probs[h, blk, r0 - c0_ : r0 - c0_ + 128, 0 : r0 - c0_ + 128]
-            out = dot(near, vh[c0_ : r0 + 128], 1, 0) + cross[r0 : r0 + 128]
-            own_v[r0 : r0 + 128, hcols(h)] = out.astype(BF)
+        for blk in (0, 1):
+            r0 = 256 * blk
+            out = dot(probs[h, blk], vh[r0 : r0 + 256], 1, 0) + cross[r0 : r0 + 256]
+            own_v[r0 : r0 + 256, hcols(h)] = out.astype(BF)
         attn_copy(h).start()
         return 0
 
@@ -429,7 +430,7 @@
                     accs[piece][zd, xd, yd, cd] = part[row : row + 16, c0_ : c0_ + width]
         return 0
 
-    run(wg_body, [(13, ev_w(4, 1))])
+    run(wg_body, [(12, ev_w(4, 1))], step=2)
     rs_start(0)
 
     for steps in wsteps:
@@ -491,18 +492,18 @@
 
         return event
 
+    run(
+        g_body,
+        [(4, starts(c0[0], c12[0])), (6, ev_c12(0)), (8, starts(c0[1], c12[1]))],
+        count=H // 2,
+    )
+
     def ev_rs(n):
         def event():
             rs_add(n)
             rs_start(n + 1)
 
         return event
-
-    run(
-        g_body,
-        [(4, starts(c0[0], c12[0])), (6, ev_c12(0)), (8, starts(c0[1], c12[1]), ev_rs(0))],
-        count=H // 2,
-    )
 
     def wait_attn(h, _):
         attn_copy(h).wait_send()
@@ -527,11 +528,13 @@
         dq = None
         prods = []
         for b in range(3):
-            pb = dot(gh, fh[128 * b : 128 * b + 128], 1, 1)
+            if b % 2 == 0:
+                pair = dot(gh, fh[128 * b : 128 * b + 256], 1, 1)
+            pb = pair[:, 128 * (b % 2) : 128 * (b % 2) + 128]
             prods.append((qf * pb).astype(BF))
             term = pb * ws[4 + b]
             dq = term if dq is None else dq + term
-        p3 = dot(gh[256:], fh[384:512], 1, 1)
+        p3 = pair[256:, 128:]
         prod3 = (qf[256:] * p3).astype(BF)
         p3 = p3 * ws[3][256:]
         far_sums = []
@@ -564,8 +567,7 @@
     run(
         dq_body,
         [
-            (2, ev_c12(1)), (5, ev_c3(0)), (7, ev_rs(1)), (12, ev_rs(2)), (13, ev_c3(1)),
-            (16, ev_rs(3)),
+            (2, ev_rs(0)), (3, ev_c12(1)), (6, ev_c3(0)), (8, ev_rs(1)), (13, ev_rs(2)), (16, ev_c3(1), ev_rs(3)),
         ],
     )
     for j in (0, 1):

time: 91.5 us -> 89 us (0.973)
  Pallas kernels: 85.4 us -> 83 us
    pallas_call x1, Pallas kernels: 85.4 us -> 83 us  [local(): pl.pallas_call(kernel, out_shape=(big, big, big, pltpu.VMEM((1, T, HD), F...]
where the time goes in v5:
time: 89 us; the launch traced here: 88.9 us
  Pallas kernels  83 us (93%)
  local copies, waits for them, and re-layouts  5.32 us (6%)
    pallas_call x1, Pallas kernels, local(): pl.pallas_call(kernel, out_shape=(big, big, big, pltpu.VMEM((1, T, HD), F...  83 us
    unnamed x5, local copies, waits for them, and re-layouts  5.32 us

profile of v5, /device:TPU:1, one launch (start us, length us, event | category | flops | bytes accessed | tf_op | source)
XLA Modules:
  0.0 88.9 jit_solution(9964946053296816974)
XLA Ops:
  0.6 83.0 %shard_map.101 = (bf16[1,512,2048]{2,1,0:T(8,128)(2,1)S(1)}, bf16[1,512,2048]{2,1,0:T(8,128)(2,1)S(1)}, bf16[1,512,2048]{2,1,0:T(8,128)(2,1)S(1)}, f32[1,512,128]{2,1,0:T(8,128)S(1)}, f32[16,2048]{1,0:T(8,128)S(1)}) custom-call(bf16[1,512,2048]{2,1,0:T(8,128)(2,1)} %q_in.1, bf16[1,512,2048]{2,1,0:T(8,128)(2,1)} %k_in.1, bf16[1,512,2048]{2,1,0:T(8,128)(2,1)} %v_in.1, ...), custom_call_target="tpu_custom_call" | custom-call | flops 20000000000 | bytes 16777216 | tf_op jit(solution)/shard_map/pallas_call | solution.py:674
  83.6 1.3 %copy.16 = bf16[1,512,2048]{2,1,0:T(8,128)(2,1)} copy(bf16[1,512,2048]{2,1,0:T(8,128)(2,1)S(1)} %get-tuple-element.5) | data formatting | bytes 4194304
  84.9 0.7 copy.20
  85.6 0.7 copy.19
  86.3 1.3 %copy.17 = bf16[1,512,2048]{2,1,0:T(8,128)(2,1)} copy(bf16[1,512,2048]{2,1,0:T(8,128)(2,1)S(1)} %get-tuple-element.6) | data formatting | bytes 4194304
  87.6 1.3 %copy.18 = bf16[1,512,2048]{2,1,0:T(8,128)(2,1)} copy(bf16[1,512,2048]{2,1,0:T(8,128)(2,1)S(1)} %get-tuple-element.7) | data formatting | bytes 4194304
